TPU v7x, 256 devices: a whole 4x4x8 slice. The times are simulated.
256 devices in a mesh: tile: 8 (over z), pos: 32 (over x, y, core).
Axes of the slice: x: 4, y: 4, z: 8, core: 2. Of those that a mesh axis runs over, the one named last changes fastest.
Arguments:
- object_field: float32 [2, 512, 4096], P(None, 'pos', 'tile'), may hold values from -6 to 6
- illumination: float32 [2, 128, 128], replicated, may hold values from -6 to 6
- row_offsets: int32 [2, 8192], P(None, ('tile', 'pos')), may hold values from 0 to 384
- col_offsets: int32 [2, 8192], P(None, ('tile', 'pos')), may hold values from 0 to 384
- counts: int32 [2, 256], P(None, ('tile', 'pos')), may hold values from 1 to 32, as said below
- amplitudes: float32 [2, 8192, 128, 128], P(None, ('tile', 'pos')), may hold values from 0.05 to 4
Outputs:
- object_out: float32 [2, 512, 4096], P(None, 'pos', 'tile')
- probe_out: float32 [2, 128, 128], replicated
Inputs may be any that keep to these rules, and one draw needn't show every extreme that they name: `counts`: in every iteration, in every strip, one device has exactly 32 live slots; a device's live slots are its first ones.
All inputs are finite; a program needn't handle non-finite values.
Results may differ from a plain program's by a relative error of at most 0.0003.
Values sent between devices are 32-bit elements; how exact they have to be, the bound alone decides.
A program may use at most 128 MiB of HBM per device.

v0:
```python
import math

import jax
import jax.numpy as jnp
from jax import lax
from jax.sharding import PartitionSpec as P

exact_mode = lax.Precision.HIGHEST
block_slots = 8


def dft_tables(width):
    ramp = jnp.arange(width, dtype=jnp.int32)
    phase = ramp[:, None] * ramp[None, :] % width
    angle = -2.0 * math.pi / width * phase.astype(jnp.float32)
    factor = 1.0 / math.sqrt(width)
    return (jnp.cos(angle) * factor, jnp.sin(angle) * factor)


def transform(real_part, imag_part, cosine, sine):
    left_real = jnp.einsum("ij,bjk->bik", cosine, real_part, precision=exact_mode) - jnp.einsum(
        "ij,bjk->bik", sine, imag_part, precision=exact_mode
    )
    left_imag = jnp.einsum("ij,bjk->bik", cosine, imag_part, precision=exact_mode) + jnp.einsum(
        "ij,bjk->bik", sine, real_part, precision=exact_mode
    )
    out_real = jnp.einsum("bij,jk->bik", left_real, cosine, precision=exact_mode) - jnp.einsum(
        "bij,jk->bik", left_imag, sine, precision=exact_mode
    )
    out_imag = jnp.einsum("bij,jk->bik", left_real, sine, precision=exact_mode) + jnp.einsum(
        "bij,jk->bik", left_imag, cosine, precision=exact_mode
    )
    return (out_real, out_imag)


def block_terms(
    object_strip, illumination, row_starts, col_starts, measured, alive_flags, cosine, sine
):
    width = illumination.shape[-1]
    anchor = jnp.zeros((), jnp.int32)
    patches = jnp.stack(
        [
            lax.dynamic_slice(
                object_strip, (anchor, row_starts[number], col_starts[number]), (2, width, width)
            )
            for number in range(row_starts.shape[0])
        ]
    )
    patch_real, patch_imag = (patches[:, 0], patches[:, 1])
    probe_real, probe_imag = (illumination[0], illumination[1])
    exit_real = probe_real * patch_real - probe_imag * patch_imag
    exit_imag = probe_real * patch_imag + probe_imag * patch_real
    far_real, far_imag = transform(exit_real, exit_imag, cosine, sine)
    modulus = jnp.sqrt(far_real * far_real + far_imag * far_imag + 1.0)
    factor = measured / modulus - 1.0
    back_real, back_imag = transform(far_real * factor, far_imag * factor, cosine, -sine)
    weights = alive_flags.astype(jnp.float32)[:, None, None]
    back_real = back_real * weights
    back_imag = back_imag * weights
    probe_power = weights * (probe_real * probe_real + probe_imag * probe_imag)[None]
    object_terms = jnp.stack(
        [
            probe_real * back_real + probe_imag * back_imag,
            probe_real * back_imag - probe_imag * back_real,
            probe_power,
        ],
        axis=1,
    )
    probe_terms = jnp.stack(
        [
            jnp.sum(patch_real * back_real + patch_imag * back_imag, axis=0),
            jnp.sum(patch_real * back_imag - patch_imag * back_real, axis=0),
            jnp.sum(weights * (patch_real * patch_real + patch_imag * patch_imag), axis=0),
        ]
    )
    return (object_terms, probe_terms)


def sweep(object_strip, illumination, row_starts, col_starts, measured, alive_flags, cosine, sine):
    width = illumination.shape[-1]
    anchor = jnp.zeros((), jnp.int32)
    blocks = row_starts.shape[0] // block_slots

    def advance(number, carry):
        begin = number * block_slots
        block_rows = lax.dynamic_slice_in_dim(row_starts, begin, block_slots)
        block_cols = lax.dynamic_slice_in_dim(col_starts, begin, block_slots)
        block_measured = lax.dynamic_slice_in_dim(measured, begin, block_slots)
        block_alive = lax.dynamic_slice_in_dim(alive_flags, begin, block_slots)

        def busy(state):
            totals, sums = state
            object_terms, probe_terms = block_terms(
                object_strip,
                illumination,
                block_rows,
                block_cols,
                block_measured,
                block_alive,
                cosine,
                sine,
            )
            for slot_number in range(block_slots):
                where_at = (anchor, block_rows[slot_number], block_cols[slot_number])
                current = lax.dynamic_slice(totals, where_at, (3, width, width))
                totals = lax.dynamic_update_slice(
                    totals, current + object_terms[slot_number], where_at
                )
            return (totals, sums + probe_terms)

        def unchanged(state):
            return state

        return lax.cond(jnp.any(block_alive > 0), busy, unchanged, carry)

    start_totals = jnp.zeros((3, object_strip.shape[1], object_strip.shape[2]), jnp.float32)
    start_sums = jnp.zeros((3, width, width), jnp.float32)
    return lax.fori_loop(0, blocks, advance, (start_totals, start_sums))


def fetch_strip(object_shard):
    return lax.all_gather(object_shard, "pos", axis=1, tiled=True)


def per_device(object_field, illumination, row_offsets, col_offsets, counts, amplitudes):
    width = illumination.shape[-1]
    cosine, sine = dft_tables(width)
    capacity = row_offsets.shape[1]
    object_strip = fetch_strip(object_field)
    for iteration in range(row_offsets.shape[0]):
        if iteration > 0:
            object_strip = fetch_strip(object_field)
        alive_flags = (jnp.arange(capacity, dtype=jnp.int32) < counts[iteration, 0]).astype(
            jnp.int32
        )
        row_starts = row_offsets[iteration]
        col_starts = col_offsets[iteration]
        measured = amplitudes[iteration]
        totals, probe_local = sweep(
            object_strip, illumination, row_starts, col_starts, measured, alive_flags, cosine, sine
        )
        probe_numer, probe_denom = lax.psum((probe_local[:2], probe_local[2]), ("tile", "pos"))
        owned = lax.psum_scatter(totals, "pos", scatter_dimension=1, tiled=True)
        denom = owned[2]
        object_field = object_field + owned[:2] / (denom + 1.0)
        illumination = illumination + probe_numer / jnp.sqrt(probe_denom + 1.0)
    return (object_field, illumination)


def solution(mesh):
    return jax.shard_map(
        per_device,
        mesh=mesh,
        in_specs=(
            P(None, "pos", "tile"),
            P(),
            P(None, ("tile", "pos")),
            P(None, ("tile", "pos")),
            P(None, ("tile", "pos")),
            P(None, ("tile", "pos"), None, None),
        ),
        out_specs=(P(None, "pos", "tile"), P()),
        check_vma=False,
    )
```

profile of v0, /device:TPU:1, one launch (start us, length us, event | category | flops | bytes accessed | tf_op | source)
XLA Modules:
  0.0 1627.3 jit_solution(12318705868814790759)
XLA Ops:
  10.7 4.8 slice_bitcast_fusion.24
  15.5 48.2 %all-gather.3.cloned.1.call-done = f32[2,512,512]{2,1,0:T(8,128)} async-done(((f32[2,16,512]{2,1,0:T(8,128)}), f32[2,512,512]{2,1,0:T(8,128)}) %all-gather.3.cloned.1.call-update) | async-done | bytes 2097168 | tf_op jit(solution)/shard_map/all_gather | solution.py:122
  63.8 2.0 broadcast.97.clone
  65.8 105.3 %while.34 = (s32[]{:T(128)}, f32[3,512,512]{2,1,0:T(8,128)}, f32[3,128,128]{2,1,0:T(8,128)S(1)}, s32[32]{0:T(128)S(1)}, s32[32]{0:T(128)S(1)}, /*index=5*/s32[32...) while((s32[]{:T(128)}, f32[3,512,512]{2,1,0:T(8,128)}, ...), condition=%wide.region_7.8_spmd.clone.clone, body=%wide.region_0.7_spmd.clone.clone.sunk | while | flops 3229433856 | bytes 43779580 | solution.py:118
  67.3 99.4 %conditional.8 = ((f32[3,512,512]{2,1,0:T(8,128)}, f32[3,128,128]{2,1,0:T(8,128)S(1)})) conditional(s32[]{:T(128)} %convert_element_type.133, (f32[3,512,512]{2,1,0:T(8,128)}, f32[3,128,128]{2,1,0:T(8,128)S(1)}) %tuple.185, (s32[32]{0:T(128)S(1)}, s32[]{:T(128)}, s32[32]{0:T(128)S(1)}, f32[3,512,512]{2,1,0:T(8,128)}, ...), branch_computations={%region_2.2_spmd, %region_3.6_spmd.clone} | conditional | flops 3229204480 | bytes 43648132 | solution.py:114
  114.7 2.1 fusion.14
  126.5 4.1 dynamic_update_slice.80
  131.7 4.0 dynamic_update_slice.81
  136.9 4.0 dynamic_update_slice.82
  142.1 4.1 dynamic_update_slice.83
  147.2 4.0 dynamic_update_slice.84
  152.4 4.0 dynamic_update_slice.85
  157.6 4.0 dynamic_update_slice.86
  162.8 3.9 dynamic_update_slice.87
  172.6 379.5 %reduce-scatter.3.cloned.1.call-done = f32[3,16,512]{2,1,0:T(8,128)} async-done(((f32[3,512,512]{2,1,0:T(8,128)}), f32[3,16,512]{2,1,0:T(8,128)}) %reduce-scatter.3.cloned.1.call-update) | async-done | bytes 98320 | tf_op jit(solution)/shard_map/reduce_scatter | solution.py:143
  555.0 251.6 %all-reduce.7.cloned.1.call-done = (f32[2,128,128]{2,1,0:T(8,128)}, f32[128,128]{1,0:T(8,128)}) async-done(((f32[2,128,128]{2,1,0:T(8,128)}, f32[128,128]{1,0:T(8,128)}), (f32[2,128,128]{2,1,0:T(8,128)}, f32[128,128]{1,0:T(8,128)})) %all-reduce.7.cloned.1.call-update) | async-done | bytes 196624 | tf_op jit(solution)/shard_map/psum | solution.py:142
  808.5 49.6 %all-gather.5.cloned.1.call-done = f32[2,512,512]{2,1,0:T(8,128)} async-done(((f32[2,16,512]{2,1,0:T(8,128)}), f32[2,512,512]{2,1,0:T(8,128)}) %all-gather.5.cloned.1.call-update) | async-done | bytes 2097168 | tf_op jit(solution)/shard_map/all_gather | solution.py:122
  858.0 2.0 broadcast.97
  860.1 121.6 %while.35 = (s32[]{:T(128)}, f32[3,512,512]{2,1,0:T(8,128)}, f32[3,128,128]{2,1,0:T(8,128)S(1)}, s32[32]{0:T(128)S(1)}, s32[32]{0:T(128)S(1)}, /*index=5*/s32[32...) while((s32[]{:T(128)}, f32[3,512,512]{2,1,0:T(8,128)}, ...), condition=%wide.region_18.19_spmd.clone.clone, body=%wide.region_11.18_spmd.clone.clone.sunk | while | flops 3229433856 | bytes 43779580 | solution.py:118
  876.8 100.2 %conditional.9 = ((f32[3,512,512]{2,1,0:T(8,128)}, f32[3,128,128]{2,1,0:T(8,128)S(1)})) conditional(s32[]{:T(128)} %convert_element_type.135, (f32[3,512,512]{2,1,0:T(8,128)}, f32[3,128,128]{2,1,0:T(8,128)S(1)}) %tuple.189, (s32[32]{0:T(128)S(1)}, s32[]{:T(128)}, s32[32]{0:T(128)S(1)}, f32[3,512,512]{2,1,0:T(8,128)}, ...), branch_computations={%region_13.13_spmd, %region_14.17_spmd.clone} | conditional | flops 3229204480 | bytes 43648132 | solution.py:114
  924.9 2.1 fusion.53
  936.7 4.0 dynamic_update_slice.88
  941.9 4.1 dynamic_update_slice.89
  947.1 4.0 dynamic_update_slice.90
  952.3 4.0 dynamic_update_slice.91
  957.4 4.1 dynamic_update_slice.92
  962.6 4.0 dynamic_update_slice.93
  967.8 4.0 dynamic_update_slice.94
  973.0 4.0 dynamic_update_slice.95
  983.6 545.0 %all-reduce.5.cloned.1.call-done = (f32[2,128,128]{2,1,0:T(8,128)}, f32[128,128]{1,0:T(8,128)}) async-done(((f32[2,128,128]{2,1,0:T(8,128)}, f32[128,128]{1,0:T(8,128)}), (f32[2,128,128]{2,1,0:T(8,128)}, f32[128,128]{1,0:T(8,128)})) %all-reduce.5.cloned.1.call-update) | async-done | bytes 196624 | tf_op jit(solution)/shard_map/psum | solution.py:142
  1529.4 1.6 divide_add_fusion
  1531.0 86.9 %reduce-scatter.5.cloned.1.call-done = f32[3,16,512]{2,1,0:T(8,128)} async-done(((f32[3,512,512]{2,1,0:T(8,128)}), f32[3,16,512]{2,1,0:T(8,128)}) %reduce-scatter.5.cloned.1.call-update) | async-done | bytes 98320 | tf_op jit(solution)/shard_map/reduce_scatter | solution.py:143
  (147 shorter events, 91.5 us)
Async XLA Ops:
  7.2 56.6 %all-gather.3.cloned.1.call-start = ((), (), s32[]{:S(2)}) async-start(), calls=%async_computation.2 | async-start | bytes 2162688 | tf_op jit(solution)/shard_map/all_gather | solution.py:122
  7.9 544.2 %reduce-scatter.3.cloned.1.call-start = ((), (), s32[]{:S(2)}) async-start(), calls=%async_computation.3 | async-start | bytes 3244032 | tf_op jit(solution)/shard_map/reduce_scatter | solution.py:143
  15.5 50.3 %copy-start = (f32[2,128,128]{2,1,0:T(8,128)S(1)}, f32[2,128,128]{2,1,0:T(8,128)}, u32[]{:S(2)}) copy-start(f32[2,128,128]{2,1,0:T(8,128)} %param.15) | copy-start | bytes 393220
  171.1 381.7 %copy-start.2 = (f32[2,16,512]{2,1,0:T(8,128)S(1)}, f32[2,16,512]{2,1,0:T(8,128)}, u32[]{:S(2)}) copy-start(f32[2,16,512]{2,1,0:T(8,128)} %param.14) | copy-start | bytes 196612
  171.2 635.5 %all-reduce.7.cloned.1.call-start = ((), (), s32[]{:S(2)}) async-start(), calls=%async_computation.7 | async-start | bytes 393216 | tf_op jit(solution)/shard_map/psum | solution.py:142
  172.5 685.5 %all-gather.5.cloned.1.call-start = ((), (), s32[]{:S(2)}) async-start(), calls=%async_computation.4 | async-start | bytes 2162688 | tf_op jit(solution)/shard_map/all_gather | solution.py:122
  554.4 974.2 %all-reduce.5.cloned.1.call-start = ((), (), s32[]{:S(2)}) async-start(), calls=%async_computation.6 | async-start | bytes 393216 | tf_op jit(solution)/shard_map/psum | solution.py:142
  982.3 636.3 %copy-start.1 = (f32[2,16,512]{2,1,0:T(8,128)S(1)}, f32[2,16,512]{2,1,0:T(8,128)}, u32[]{:S(2)}) copy-start(f32[2,16,512]{2,1,0:T(8,128)} %fusion.87) | copy-start | bytes 196612
  983.0 634.9 %reduce-scatter.5.cloned.1.call-start = ((), (), s32[]{:S(2)}) async-start(), calls=%async_computation.5 | async-start | bytes 3244032 | tf_op jit(solution)/shard_map/reduce_scatter | solution.py:143
Sparse Core Ops, SparseCore 0:
  10.7 53.0 all-gather.2
  171.3 380.7 reduce-scatter.2
  559.1 247.4 all-reduce.6
  810.1 47.8 all-gather.4
  983.1 545.3 all-reduce.4
  1532.8 84.9 reduce-scatter.4
where the time goes:
time: 1660 us; the launch traced here: 1630 us
  waiting for transfers between devices  1360 us (82%)
  local copies, waits for them, and re-layouts  98.4 us (6%)
  loops' own time  81.5 us (5%)
  other arithmetic  36.1 us (2%)
  matrix products  34.5 us (2%)
    psum x2, waiting for transfers between devices, per_device(): lax.psum((probe_local[:2], probe_local[2]), ('tile', 'pos'))  797 us
    reduce_scatter x2, waiting for transfers between devices, per_device(): owned = lax.psum_scatter(totals, 'pos', scatter_dimension=1, tiled=True)  466 us
    all_gather x2, waiting for transfers between devices, fetch_strip(): return lax.all_gather(object_shard, 'pos', axis=1, tiled=True)  97.8 us
    dynamic_update_slice x16, local copies, waits for them, and re-layouts, busy(): lax.dynamic_update_slice(totals, current + object_terms[slot_number], whe...  64.6 us
    another operation x8, loops' own time, advance(): return lax.cond(jnp.any(block_alive > 0), busy, unchanged, carry)  60.9 us
  transfers between devices with their start and end apart: 6, of which 6 were waited for; matrix products, arithmetic and copies ran while one was open for 1% of the time, Pallas kernels for 0%

commit v1 on v0

v1 whole, which is shorter than its diff:
```python
import functools
import math

import jax
import jax.numpy as jnp
import ml_dtypes
import numpy as np
from jax import lax
from jax.experimental import pallas as pl
from jax.experimental.pallas import tpu as pltpu
from jax.sharding import PartitionSpec as P

WIN = 128
ROWS = 512
GROUPS = ROWS // 8
COLS = ROWS // WIN
PTILES = 3 * WIN // 8
BLOCK = 4
RING = 4
MESH = pl.DeviceIdType.MESH
f32 = jnp.float32


def transform_tables():
    ramp = np.arange(WIN)
    angle = -2.0 * np.pi / WIN * (np.outer(ramp, ramp) % WIN)
    c, s = np.cos(angle) / math.sqrt(WIN), np.sin(angle) / math.sqrt(WIN)
    pairs = []
    for matrix in (np.block([[c, s], [-s, c]]), np.block([[c, -s], [s, c]])):
        high = matrix.astype(ml_dtypes.bfloat16)
        low = (matrix - high.astype(np.float64)).astype(ml_dtypes.bfloat16)
        pairs.append((high, low))
    (ah, al), (bh, bl) = pairs
    right = np.stack([np.concatenate([ah, ah, al]), np.concatenate([bh, bh, bl])])
    left = np.stack([np.concatenate([bh, bh, bl], 1), np.concatenate([ah, ah, al], 1)])
    return right, left


def split(x):
    high = x.astype(jnp.bfloat16)
    return high, (x - high.astype(f32)).astype(jnp.bfloat16)


def transform(pairs, right, left):
    halves = [[split(part) for part in pair] for pair in pairs]
    high, low = (
        jnp.concatenate([jnp.concatenate([re[k], im[k]], 1) for re, im in halves], 0) for k in range(2)
    )
    y = jnp.dot(jnp.concatenate([high, low, high], 1), right, preferred_element_type=f32)
    out = []
    for k in range(0, len(pairs), 2):
        quarters = [
            [split(y[(k + j) * WIN : (k + j + 1) * WIN, p * WIN : (p + 1) * WIN]) for j in range(2)]
            for p in range(2)
        ]
        high, low = (
            jnp.concatenate([jnp.concatenate([q[n] for q in row], 1) for row in quarters], 0) for n in range(2)
        )
        z = jnp.dot(left, jnp.concatenate([high, low, high], 0), preferred_element_type=f32)
        for j in range(2):
            out.append((z[:WIN, j * WIN : (j + 1) * WIN], z[WIN:, j * WIN : (j + 1) * WIN]))
    return out


def probe_step(probe, sums):
    scale = lax.rsqrt(sums[2] + 1.0)
    return [probe[k] + (sums[k] - probe[k] * sums[2]) * scale for k in range(2)]


def sweep_kernel(
    iteration, rows_hbm, cols_hbm, counts_hbm, probe_hbm, right_hbm, left_hbm, strip_hbm, amp_hbm,
    out_hbm, probe_out,
    rows, cols, counts, right, left, probe, old_sums, strip, sums, amp, probe_sums, small_sem, strip_sem, amp_sem, out_sem,
):
    cap = rows.shape[1]
    n_blocks = cap // BLOCK
    updates = strip_hbm.shape[1] > 2 * COLS
    copies = [
        pltpu.make_async_copy(src, dst, small_sem.at[k])
        for k, (src, dst) in enumerate(
            [(counts_hbm, counts), (rows_hbm, rows), (cols_hbm, cols), (probe_hbm, probe), (right_hbm, right), (left_hbm, left)]
        )
    ]
    if updates:
        copies.append(pltpu.make_async_copy(strip_hbm.at[pl.ds(0, PTILES), 2 * COLS], old_sums, small_sem.at[6]))
    copies += [pltpu.make_async_copy(strip_hbm.at[:, k], strip.at[k], strip_sem.at[k]) for k in range(2 * COLS)]
    for copy in copies:
        copy.start()

    def amp_copy(k):
        part = pl.ds(k * BLOCK, BLOCK)
        return pltpu.make_async_copy(amp_hbm.at[iteration, part], amp.at[part], amp_sem.at[k])

    for k in range(n_blocks):
        amp_copy(k).start()
    sums_rows = sums.reshape(3 * COLS, ROWS, WIN)
    strip_rows = strip.reshape(2 * COLS, ROWS, WIN)
    probe_rows = probe_sums.reshape(ROWS // WIN, WIN, WIN)
    for k in range(3 * COLS):
        sums_rows[k] = jnp.zeros((ROWS, WIN), f32)
    for k in range(ROWS // WIN):
        probe_rows[k] = jnp.zeros((WIN, WIN), f32)
    for copy in copies:
        copy.wait()
    if updates:
        stepped = probe_step(probe, old_sums.reshape(3, WIN, WIN))
        for k in range(2):
            probe[k] = stepped[k]
    probe_out[...] = probe[...]
    count = counts[iteration, 0]
    lane = lax.broadcasted_iota(jnp.int32, (WIN, WIN), 1)
    trips = (count + BLOCK - 1) // BLOCK

    def body(k, carry):
        amp_copy(k).wait()
        held, exits = [], []
        for j in range(BLOCK):
            slot = k * BLOCK + j
            row, col = rows[iteration, slot], cols[iteration, slot]
            first, turn = col // WIN, col % WIN
            second = jnp.minimum(first + 1, COLS - 1)
            here = lane >= turn
            window = pl.ds(row, WIN)
            q = [
                jnp.where(here, strip_rows[COLS * p + first, window, :], strip_rows[COLS * p + second, window, :])
                for p in range(2)
            ]
            pr = [pltpu.roll(probe[p], turn, 1) for p in range(2)]
            exits.append((pr[0] * q[0] - pr[1] * q[1], pr[0] * q[1] + pr[1] * q[0]))
            held.append((slot, window, first, second, turn, here, q, pr))
        scaled = []
        for (slot, *_), (re, im) in zip(held, transform(exits, right[0], left[0])):
            factor = amp[slot] * lax.rsqrt(re * re + im * im + 1.0)
            factor = jnp.where(slot < count, factor, 0.0)
            scaled.append((re * factor, im * factor))
        for (slot, window, first, second, turn, here, (qr, qi), (pr, pi)), (gr, gi) in zip(
            held, transform(scaled, right[1], left[1])
        ):
            live = (slot < count).astype(f32)
            for p, term in enumerate((pr * gr + pi * gi, pr * gi - pi * gr, (pr * pr + pi * pi) * live)):
                sums_rows[COLS * p + first, window, :] += jnp.where(here, term, 0.0)
                sums_rows[COLS * p + second, window, :] += jnp.where(here, 0.0, term)
            back = jnp.where(turn == 0, 0, WIN - turn)
            for p, term in enumerate((qr * gr + qi * gi, qr * gi - qi * gr, (qr * qr + qi * qi) * live)):
                probe_rows[p] += pltpu.roll(term, back, 1)
        return carry

    lax.fori_loop(0, trips, body, 0)

    def drain(k, carry):
        amp_copy(k).wait()
        return carry

    lax.fori_loop(trips, n_blocks, drain, 0)
    outs = [pltpu.make_async_copy(sums.at[k], out_hbm.at[:, k], out_sem.at[k]) for k in range(3 * COLS)]
    outs.append(pltpu.make_async_copy(probe_sums, out_hbm.at[:, 3 * COLS], out_sem.at[3 * COLS]))
    for copy in outs:
        copy.start()
    for copy in outs:
        copy.wait()


ANY = pl.BlockSpec(memory_space=pl.ANY)
VMEM = pl.BlockSpec(memory_space=pltpu.VMEM)


def sweep(iteration, strip, probe, rows, cols, counts, amplitudes, right, left):
    cap = rows.shape[1]
    return pl.pallas_call(
        functools.partial(sweep_kernel, iteration),
        out_shape=(
            jax.ShapeDtypeStruct((GROUPS, 3 * COLS + 1, 8, WIN), f32),
            jax.ShapeDtypeStruct(probe.shape, f32),
        ),
        in_specs=[ANY] * 8,
        out_specs=(ANY, VMEM),
        scratch_shapes=[
            pltpu.SMEM(rows.shape, jnp.int32),
            pltpu.SMEM(cols.shape, jnp.int32),
            pltpu.SMEM(counts.shape, jnp.int32),
            pltpu.VMEM(right.shape, jnp.bfloat16),
            pltpu.VMEM(left.shape, jnp.bfloat16),
            pltpu.VMEM(probe.shape, f32),
            pltpu.VMEM((PTILES, 8, WIN), f32),
            pltpu.VMEM((2 * COLS, GROUPS, 8, WIN), f32),
            pltpu.VMEM((3 * COLS, GROUPS, 8, WIN), f32),
            pltpu.VMEM((cap, WIN, WIN), f32),
            pltpu.VMEM((GROUPS, 8, WIN), f32),
            pltpu.SemaphoreType.DMA((7,)),
            pltpu.SemaphoreType.DMA((2 * COLS,)),
            pltpu.SemaphoreType.DMA((cap // BLOCK,)),
            pltpu.SemaphoreType.DMA((3 * COLS + 1,)),
        ],
        compiler_params=pltpu.CompilerParams(vmem_limit_bytes=40 * 1024 * 1024),
        name="sweep",
    )(rows, cols, counts, probe, right, left, strip, amplitudes)


class Place:
    def __init__(self):
        pos = lax.axis_index("pos")
        self.tile = lax.axis_index("tile")
        core, y, x = pos % 2, pos // 2 % RING, pos // (2 * RING)
        self.core = core
        self.near, self.far = x + core * (y - x), y + core * (x - y)
        self.near_step, self.far_step = 8 - 6 * core, 2 + 6 * core

    def at(self, near, far):
        return (self.near + near) % RING * self.near_step + (self.far + far) % RING * self.far_step + self.core

    def other_at(self, near, far):
        return (self.far + near) % RING * self.far_step + (self.near + far) % RING * self.near_step + 1 - self.core

    def partners(self):
        return [self.at(1, 0), self.at(3, 0), self.at(0, 1), self.at(0, 3), self.other_at(0, 0)]


def greet(place, with_tiles):
    barrier = pltpu.get_barrier_semaphore()
    for partner in place.partners():
        pl.semaphore_signal(barrier, inc=1, device_id={"pos": partner}, device_id_type=MESH)
    tiles = lax.axis_size("tile") if with_tiles else 1
    for k in range(1, tiles):
        pl.semaphore_signal(barrier, inc=1, device_id={"tile": (place.tile + k) % tiles}, device_id_type=MESH)
    pl.semaphore_wait(barrier, len(place.partners()) + tiles - 1)


class Sender:
    def __init__(self, send_sem, recv_sem):
        self.send_sem, self.recv_sem = send_sem, recv_sem
        self.names, self.sent = {}, []

    def slot(self, name):
        return self.names.setdefault(name, len(self.names))

    def copy(self, name, src, dst, device):
        k = self.slot(name)
        return pltpu.make_async_remote_copy(
            src_ref=src, dst_ref=dst, send_sem=self.send_sem.at[k], recv_sem=self.recv_sem.at[k],
            device_id=device, device_id_type=MESH,
        )

    def send(self, name, src, dst, device):
        copy = self.copy(name, src, dst, device)
        copy.start()
        self.sent.append(copy)

    def arrive(self, name, dst, device):
        self.copy(name, dst, dst, device).wait_recv()

    def finish(self):
        for copy in self.sent:
            copy.wait_send()


def gather(place, sender, buf):
    np_, nm, fp, fm, other = [{"pos": p} for p in place.partners()]

    def both(near, far):
        return buf.at[pl.ds(2 * place.at(near, far), 2)]

    def half(near, far, k):
        return buf.at[2 * place.at(near, far) + k]

    def pass_on(near):
        sender.send(("f+", near), both(near, 0), both(near, 0), fp)
        sender.send(("f-", near), both(near, 0), both(near, 0), fm)

    def to_other(near, far):
        sender.send(("core", near, far), both(near, far), both(near, far), other)

    sender.send("n+", both(0, 0), both(0, 0), np_)
    sender.send("n-", both(0, 0), both(0, 0), nm)
    pass_on(0)
    to_other(0, 0)
    sender.arrive("n+", both(3, 0), nm)
    sender.send("n++", half(3, 0, 0), half(3, 0, 0), np_)
    pass_on(3)
    sender.arrive("n-", both(1, 0), np_)
    sender.send("n--", half(1, 0, 1), half(1, 0, 1), nm)
    pass_on(1)
    to_other(3, 0)
    to_other(1, 0)

    def relay(near):
        sender.arrive(("f+", near), both(near, 3), fm)
        sender.send(("f++", near), half(near, 3, 0), half(near, 3, 0), fp)
        to_other(near, 3)
        sender.arrive(("f-", near), both(near, 1), fp)
        sender.send(("f--", near), half(near, 1, 1), half(near, 1, 1), fm)
        to_other(near, 1)

    relay(0)
    sender.arrive("n++", half(2, 0, 0), nm)
    sender.arrive("n--", half(2, 0, 1), np_)
    pass_on(2)
    to_other(2, 0)
    for near in (3, 1, 2):
        relay(near)
    for near in (0, 3, 1, 2):
        sender.arrive(("f++", near), half(near, 2, 0), fm)
        sender.arrive(("f--", near), half(near, 2, 1), fp)
        to_other(near, 2)
    for near, far in core_order:
        at = buf.at[pl.ds(2 * place.other_at(near, far), 2)]
        sender.arrive(("core", near, far), at, other)


core_order = [(0, 0), (3, 0), (1, 0), (0, 3), (0, 1), (2, 0)]
core_order += [(n, f) for n in (3, 1, 2) for f in (3, 1)] + [(n, 2) for n in (0, 3, 1, 2)]


def reduce(place, sender, sums_hbm, own, core_in, far_half, far_full, near_half, near_full, load_sem):
    np_, nm, fp, fm, other = [{"pos": p} for p in place.partners()]
    order = [(near, far) for far in (2, 1, 3, 0) for near in (2, 1, 3, 0)]
    loads = {}
    for near, far in order:
        k = 4 * near + far
        sender.send(("core", near, far), sums_hbm.at[pl.ds(2 * place.other_at(near, far), 2)], core_in.at[near, far], other)
        loads[near, far] = pltpu.make_async_copy(
            sums_hbm.at[pl.ds(2 * place.at(near, far), 2)], own.at[near, far], load_sem.at[k]
        )
        loads[near, far].start()

    def pair(near, far):
        loads[near, far].wait()
        sender.arrive(("core", near, far), core_in.at[near, far], other)
        own[near, far] += core_in[near, far]

    for near in (2, 1, 3, 0):
        pair(near, 2)
        sender.send(("f++", near), own.at[near, 2, 0], far_half.at[near, 0], fp)
        sender.send(("f--", near), own.at[near, 2, 1], far_half.at[near, 1], fm)
    for near in (2, 1, 3, 0):
        pair(near, 1)
        sender.arrive(("f++", near), far_half.at[near, 0], fm)
        own[near, 1, 0] += far_half[near, 0]
        sender.send(("f+", near), own.at[near, 1], far_full.at[near, 0], fp)
        pair(near, 3)
        sender.arrive(("f--", near), far_half.at[near, 1], fp)
        own[near, 3, 1] += far_half[near, 1]
        sender.send(("f-", near), own.at[near, 3], far_full.at[near, 1], fm)

    def line(near):
        pair(near, 0)
        sender.arrive(("f+", near), far_full.at[near, 0], fm)
        sender.arrive(("f-", near), far_full.at[near, 1], fp)
        own[near, 0] += far_full[near, 0] + far_full[near, 1]

    line(2)
    sender.send("n++", own.at[2, 0, 0], near_half.at[0], np_)
    sender.send("n--", own.at[2, 0, 1], near_half.at[1], nm)
    line(1)
    sender.arrive("n++", near_half.at[0], nm)
    own[1, 0, 0] += near_half[0]
    sender.send("n+", own.at[1, 0], near_full.at[0], np_)
    line(3)
    sender.arrive("n--", near_half.at[1], np_)
    own[3, 0, 1] += near_half[1]
    sender.send("n-", own.at[3, 0], near_full.at[1], nm)
    line(0)
    sender.arrive("n+", near_full.at[0], nm)
    sender.arrive("n-", near_full.at[1], np_)
    own[0, 0] += near_full[0] + near_full[1]


def across(place, sender, mine, seen):
    tiles = seen.shape[0]
    seen[place.tile] = mine
    for k in range(1, tiles):
        to = (place.tile + k) % tiles
        sender.send(("tile", k), seen.at[place.tile], seen.at[place.tile], {"tile": to})
    for k in range(1, tiles):
        source = (place.tile + tiles - k) % tiles
        sender.arrive(("tile", k), seen.at[source], {"tile": source})
    total = seen[0]
    for k in range(1, tiles):
        total = total + seen[k]
    return total


def gather_kernel(object_ref, out_hbm, mine, send_sem, recv_sem, copy_sem):
    place = Place()
    for g in range(2):
        for p in range(2):
            for b in range(COLS):
                mine[g, COLS * p + b] = object_ref[p, 8 * g : 8 * g + 8, WIN * b : WIN * b + WIN]
    own = out_hbm.at[pl.ds(2 * place.at(0, 0), 2)]
    copy = pltpu.make_async_copy(mine, own, copy_sem)
    copy.start()
    greet(place, False)
    copy.wait()
    sender = Sender(send_sem, recv_sem)
    gather(place, sender, out_hbm)
    sender.finish()


def object_step(old, sums):
    for g in range(2):
        for b in range(COLS):
            scale = 1.0 / (sums[g, 2 * COLS + b] + 1.0)
            for p in range(2):
                yield g, p, b, (old[g, COLS * p + b] + sums[g, COLS * p + b]) * scale


def middle_kernel(
    sums_hbm, strip_hbm, out_hbm,
    old, own, core_in, far_half, far_full, near_half, near_full, seen, mine,
    load_sem, copy_sem, send_sem, recv_sem, send_sem2, recv_sem2,
):
    place = Place()
    here = pl.ds(2 * place.at(0, 0), 2)
    load = pltpu.make_async_copy(strip_hbm.at[here, pl.ds(0, 2 * COLS)], old, copy_sem)
    load.start()
    greet(place, True)
    first, second = Sender(send_sem, recv_sem), Sender(send_sem2, recv_sem2)
    reduce(place, first, sums_hbm, own, core_in, far_half, far_full, near_half, near_full, load_sem)
    total = own.at[0, 0]
    load.wait()
    for g, p, b, tile in object_step(old, total):
        mine[g, COLS * p + b] = tile
    mine[:, 2 * COLS] = across(place, first, total[:, 3 * COLS], seen)
    copy = pltpu.make_async_copy(mine, out_hbm.at[here], copy_sem)
    copy.start()
    copy.wait()
    gather(place, second, out_hbm)
    first.finish()
    second.finish()


def last_kernel(
    sums_hbm, strip_hbm, probe_ref, object_out, probe_out,
    old, own, core_in, far_half, far_full, near_half, near_full, seen, probe_sums,
    load_sem, copy_sem, send_sem, recv_sem, send_sem2, recv_sem2,
):
    place = Place()
    here = pl.ds(2 * place.at(0, 0), 2)
    load = pltpu.make_async_copy(strip_hbm.at[here, pl.ds(0, 2 * COLS)], old, copy_sem)
    load.start()
    greet(place, True)
    first, second = Sender(send_sem, recv_sem), Sender(send_sem2, recv_sem2)
    reduce(place, first, sums_hbm, own, core_in, far_half, far_full, near_half, near_full, load_sem)
    total = own.at[0, 0]
    probe_sums[here] = across(place, first, total[:, 3 * COLS], seen)
    load.wait()
    for g, p, b, tile in object_step(old, total):
        object_out[p, 8 * g : 8 * g + 8, WIN * b : WIN * b + WIN] = tile
    gather(place, second, probe_sums)
    stepped = probe_step(probe_ref, probe_sums.reshape(ROWS // WIN, WIN, WIN))
    for k in range(2):
        probe_out[k] = stepped[k]
    first.finish()
    second.finish()


GATHER_COPIES, REDUCE_COPIES = 36, 36


def dma(n):
    return pltpu.SemaphoreType.DMA((n,))


def reduce_scratch(tiles):
    chunk = (2, 3 * COLS + 1, 8, WIN)
    return [
        pltpu.VMEM((2, 2 * COLS, 8, WIN), f32),
        pltpu.VMEM((RING, RING) + chunk, f32),
        pltpu.VMEM((RING, RING) + chunk, f32),
        pltpu.VMEM((RING,) + chunk, f32),
        pltpu.VMEM((RING, 2) + chunk, f32),
        pltpu.VMEM(chunk, f32),
        pltpu.VMEM((2,) + chunk, f32),
        pltpu.VMEM((tiles, 2, 8, WIN), f32),
    ]


def params(collective_id):
    return pltpu.CompilerParams(
        collective_id=collective_id, has_side_effects=True, vmem_limit_bytes=40 * 1024 * 1024
    )


def gather_object(object_field):
    return pl.pallas_call(
        gather_kernel,
        out_shape=jax.ShapeDtypeStruct((GROUPS, 2 * COLS, 8, WIN), f32),
        in_specs=[VMEM],
        out_specs=ANY,
        scratch_shapes=[
            pltpu.VMEM((2, 2 * COLS, 8, WIN), f32), dma(GATHER_COPIES), dma(GATHER_COPIES), pltpu.SemaphoreType.DMA,
        ],
        compiler_params=params(0),
        name="gather_object",
    )(object_field)


def exchange_sems(tiles):
    copies = REDUCE_COPIES + tiles - 1
    return [
        dma(RING * RING), pltpu.SemaphoreType.DMA,
        dma(copies), dma(copies), dma(GATHER_COPIES), dma(GATHER_COPIES),
    ]


def middle(sums, strip):
    tiles = lax.axis_size("tile")
    return pl.pallas_call(
        middle_kernel,
        out_shape=jax.ShapeDtypeStruct((GROUPS, 2 * COLS + 1, 8, WIN), f32),
        in_specs=[ANY, ANY],
        out_specs=ANY,
        scratch_shapes=reduce_scratch(tiles) + [pltpu.VMEM((2, 2 * COLS + 1, 8, WIN), f32)] + exchange_sems(tiles),
        compiler_params=params(1),
        name="exchange_middle",
    )(sums, strip)


def last(sums, strip, probe, object_shape):
    tiles = lax.axis_size("tile")
    return pl.pallas_call(
        last_kernel,
        out_shape=(jax.ShapeDtypeStruct(object_shape, f32), jax.ShapeDtypeStruct(probe.shape, f32)),
        in_specs=[ANY, ANY, VMEM],
        out_specs=(VMEM, VMEM),
        scratch_shapes=reduce_scratch(tiles) + [pltpu.VMEM((GROUPS, 8, WIN), f32)] + exchange_sems(tiles),
        compiler_params=params(2),
        name="exchange_last",
    )(sums, strip, probe)


def per_device(object_field, illumination, row_offsets, col_offsets, counts, amplitudes):
    right, left = (jnp.asarray(table) for table in transform_tables())
    strip, probe = gather_object(object_field), illumination
    iterations = row_offsets.shape[0]
    for iteration in range(iterations):
        sums, probe = sweep(iteration, strip, probe, row_offsets, col_offsets, counts, amplitudes, right, left)
        if iteration + 1 < iterations:
            strip = middle(sums, strip)
    return last(sums, strip, probe, object_field.shape)


def solution(mesh):
    return jax.shard_map(
        per_device,
        mesh=mesh,
        in_specs=(
            P(None, "pos", "tile"),
            P(),
            P(None, ("tile", "pos")),
            P(None, ("tile", "pos")),
            P(None, ("tile", "pos")),
            P(None, ("tile", "pos"), None, None),
        ),
        out_specs=(P(None, "pos", "tile"), P()),
        check_vma=False,
    )
```

time: 1660 us -> 153 us (0.09); the launches traced: 1630 us -> 152 us
  waiting for transfers between devices: 1360 us -> 0 us
  Pallas kernels: 0 us -> 142 us
  local copies, waits for them, and re-layouts: 98.4 us -> 9.6 us
  loops' own time: 81.5 us -> 0 us
  other arithmetic: 36.1 us -> 0 us
  matrix products: 34.5 us -> 0 us
    psum x2 -> x0, waiting for transfers between devices: 797 us -> none  [per_device(): lax.psum((probe_local[:2], probe_local[2]), ('tile', 'pos'))]
    reduce_scatter x2 -> x0, waiting for transfers between devices: 466 us -> none  [per_device(): owned = lax.psum_scatter(totals, 'pos', scatter_dimension=1, tiled=True)]
    pallas_call x0 -> x5, Pallas kernels: none -> 142 us  [the longest x1 51.8 us: last(): pl.pallas_call(last_kernel, out_shape=(jax.ShapeDtypeStruct(object_shape,...]
    all_gather x2 -> x0, waiting for transfers between devices: 97.8 us -> none  [fetch_strip(): return lax.all_gather(object_shard, 'pos', axis=1, tiled=True)]
    another operation x10 -> x0, loops' own time: 81.5 us -> none  [the longest x8 60.9 us: advance(): return lax.cond(jnp.any(block_alive > 0), busy, unchanged, carry)]
    dynamic_update_slice x16 -> x0, local copies, waits for them, and re-layouts: 64.6 us -> none  [busy(): lax.dynamic_update_slice(totals, current + object_terms[slot_number], whe...]
    dot_general x32 -> x0, matrix products: 34.5 us -> none  [the longest x4 6.1 us: transform(): jnp.einsum('bij,jk->bik', left_imag, cosine, precision=exact_mode)]
    add x20 -> x0, other arithmetic: 23.6 us -> none  [the longest x16 18.2 us: busy(): current + object_terms[slot_number]]
  transfers between devices with their start and end apart: 6 -> 0, of which waited for: 6 -> 0; matrix products, arithmetic and copies ran while one was open for 1% -> 0% of each run, Pallas kernels for 0% -> 0%
where the time goes in v1:
time: 153 us; the launch traced here: 152 us
  Pallas kernels  142 us (93%)
  local copies, waits for them, and re-layouts  9.6 us (6%)
    pallas_call x1, Pallas kernels, last(): pl.pallas_call(last_kernel, out_shape=(jax.ShapeDtypeStruct(object_shape,...  51.8 us
    pallas_call x1, Pallas kernels, middle(): pl.pallas_call(middle_kernel, out_shape=jax.ShapeDtypeStruct((GROUPS, 2 *...  51.5 us
    pallas_call x1, Pallas kernels, gather_object(): pl.pallas_call(gather_kernel, out_shape=jax.ShapeDtypeStruct((GROUPS, 2 *...  20.2 us
    pallas_call x2, Pallas kernels, sweep(): pl.pallas_call(functools.partial(sweep_kernel, iteration), out_shape=(jax...  18.5 us
    unnamed x23, local copies, waits for them, and re-layouts  9.6 us

profile of v1, /device:TPU:1, one launch (start us, length us, event | category | flops | bytes accessed | tf_op | source)
XLA Modules:
  0.0 152.3 jit_solution(7331376609560722772)
XLA Ops:
  0.6 0.7 copy.11.counts_hbm
  1.4 0.0 copy-start.7
  1.4 0.8 copy-done.7
  2.2 20.2 %gather_object.1.strip_hbm = f32[64,8,8,128]{3,2,1,0:T(8,128)S(1)} custom-call(f32[2,16,512]{2,1,0:T(8,128)S(1)} %copy-done.7), custom_call_target="tpu_custom_call" | custom-call | tf_op jit(solution)/shard_map/gather_object/pallas_call | solution.py:484
  22.4 0.0 copy-start
  22.4 2.2 %copy-done = f32[2,32,128,128]{3,2,1,0:T(8,128)S(1)} copy-done((f32[2,32,128,128]{3,2,1,0:T(8,128)S(1)}, f32[2,32,128,128]{3,2,1,0:T(8,128)}, u32[]{:S(2)}) %copy-start) | copy-done | bytes 4194328
  24.6 0.0 copy-start.2
  24.6 1.1 copy-done.2
  25.7 0.0 copy-start.4
  25.7 1.1 copy-done.4
  26.9 0.0 copy-start.6
  26.9 0.9 copy-done.6
  27.8 0.0 copy-start.8
  27.8 0.7 copy-done.8
  28.4 0.0 copy-start.9
  28.4 0.7 copy-done.9
  29.1 12.6 %sweep.2 = (f32[64,13,8,128]{3,2,1,0:T(8,128)S(1)}, f32[2,128,128]{2,1,0:T(8,128)S(1)}) custom-call(s32[2,32]{1,0:T(2,128)S(1)} %copy-done.8, s32[2,32]{1,0:T(2,128)S(1)} %copy-done.9, s32[2,1]{1,0:T(2,128)S(1)} %copy.11.counts_hbm, f32[2,128,128]{2,1,0:T(8,128)S(1)} %copy-done.6, bf16[2,768,256]{2,1,0:T(8,128)(2,1)S(1)} %copy-done.4, ...), custom_call_target="tpu_custom_call" | custom-call | tf_op jit(solution)/shard_map/sweep/pallas_call | solution.py:169
  41.7 0.0 copy-start.1
  41.7 0.0 copy-start.3
  41.7 0.0 copy-start.5
  41.8 51.5 %exchange_middle.1.strip_hbm = f32[64,9,8,128]{3,2,1,0:T(8,128)S(1)} custom-call(f32[64,13,8,128]{3,2,1,0:T(8,128)S(1)} %get-tuple-element.7.sums_hbm, f32[64,8,8,128]{3,2,1,0:T(8,128)S(1)} %gather_object.1.strip_hbm), custom_call_target="tpu_custom_call" | custom-call | tf_op jit(solution)/shard_map/exchange_middle/pallas_call | solution.py:507
  93.3 0.0 copy-done.1
  93.3 0.0 copy-done.3
  93.3 0.0 copy-done.5
  93.3 5.9 %sweep.3 = (f32[64,13,8,128]{3,2,1,0:T(8,128)S(1)}, f32[2,128,128]{2,1,0:T(8,128)S(1)}) custom-call(s32[2,32]{1,0:T(2,128)S(1)} %copy-done.8, s32[2,32]{1,0:T(2,128)S(1)} %copy-done.9, s32[2,1]{1,0:T(2,128)S(1)} %copy.11.counts_hbm, f32[2,128,128]{2,1,0:T(8,128)S(1)} %get-tuple-element.6.probe_hbm, bf16[2,768,256]{2,1,0:T(8,128)(2,1)S(1)} %copy-done.5, ...), custom_call_target="tpu_custom_call" | custom-call | tf_op jit(solution)/shard_map/sweep/pallas_call | solution.py:169
  99.2 51.8 %exchange_last.1 = (f32[2,16,512]{2,1,0:T(8,128)S(1)}, f32[2,128,128]{2,1,0:T(8,128)S(1)}) custom-call(f32[64,13,8,128]{3,2,1,0:T(8,128)S(1)} %get-tuple-element.8.sums_hbm, f32[64,9,8,128]{3,2,1,0:T(8,128)S(1)} %exchange_middle.1.strip_hbm, f32[2,128,128]{2,1,0:T(8,128)S(1)} %get-tuple-element.9.probe_ref), custom_call_target="tpu_custom_call" | custom-call | tf_op jit(solution)/shard_map/exchange_last/pallas_call | solution.py:520
  151.0 0.6 copy.14
  151.6 0.7 copy.15
Async XLA Ops:
  1.4 0.8 copy-start.7
  22.4 2.2 %copy-start = (f32[2,32,128,128]{3,2,1,0:T(8,128)S(1)}, f32[2,32,128,128]{3,2,1,0:T(8,128)}, u32[]{:S(2)}) copy-start(f32[2,32,128,128]{3,2,1,0:T(8,128)} %amp_hbm.3) | copy-start | bytes 12582916
  24.6 1.1 copy-start.2
  25.7 1.1 copy-start.4
  26.9 0.9 copy-start.6
  27.8 0.7 copy-start.8
  28.4 0.7 copy-start.9
  41.7 51.6 %copy-start.1 = (f32[2,32,128,128]{3,2,1,0:T(8,128)S(1)}, f32[2,32,128,128]{3,2,1,0:T(8,128)}, u32[]{:S(2)}) copy-start(f32[2,32,128,128]{3,2,1,0:T(8,128)} %amp_hbm.3) | copy-start | bytes 12582916
  41.7 51.5 %copy-start.3 = (bf16[2,256,768]{2,1,0:T(8,128)(2,1)S(1)}, bf16[2,256,768]{2,1,0:T(8,128)(2,1)}, u32[]{:S(2)}) copy-start(bf16[2,256,768]{2,1,0:T(8,128)(2,1)} %constant.5.clone.left_hbm) | copy-start | bytes 2359300
  41.7 51.5 %copy-start.5 = (bf16[2,768,256]{2,1,0:T(8,128)(2,1)S(1)}, bf16[2,768,256]{2,1,0:T(8,128)(2,1)}, u32[]{:S(2)}) copy-start(bf16[2,768,256]{2,1,0:T(8,128)(2,1)} %constant.4.clone.right_hbm) | copy-start | bytes 2359300

commit v2 on v0

v2 whole, which is shorter than its diff:
```python
import functools
import math

import jax
import jax.numpy as jnp
import ml_dtypes
import numpy as np
from jax import lax
from jax.experimental import pallas as pl
from jax.experimental.pallas import tpu as pltpu
from jax.sharding import PartitionSpec as P

WIN = 128
ROWS = 512
GROUPS = ROWS // 8
COLS = ROWS // WIN
OTILES, STILES = 2 * COLS, 3 * COLS
BLOCK = 8
RING = 4
AWAY, ALL = (2, 1, 3), (2, 1, 3, 0)
MESH = pl.DeviceIdType.MESH
f32 = jnp.float32


def transform_tables():
    ramp = np.arange(WIN)
    angle = -2.0 * np.pi / WIN * (np.outer(ramp, ramp) % WIN)
    c, s = np.cos(angle) / math.sqrt(WIN), np.sin(angle) / math.sqrt(WIN)
    return np.stack([np.block([[c, s], [-s, c]]), np.block([[c, -s], [s, c]])]).astype(np.float32)


def split(x):
    high = x.astype(jnp.bfloat16)
    return high, (x - high.astype(f32)).astype(jnp.bfloat16)


def blocks(rows):
    halves = [[split(part) for part in row] for row in rows]
    return [jnp.concatenate([jnp.concatenate([part[k] for part in row], 1) for row in halves], 0) for k in range(2)]


def dot(a, b):
    return jnp.dot(a, b, preferred_element_type=f32)


def along_columns(pairs, table):
    high, low = blocks(pairs)
    both = dot(jnp.concatenate([high, low], 0), table[: 2 * WIN])
    return both[: 2 * WIN] + both[2 * WIN :] + dot(high, table[2 * WIN :])


def along_rows(y, table):
    quarter = [[y[j * WIN : (j + 1) * WIN, p * WIN : (p + 1) * WIN] for j in range(2)] for p in range(2)]
    high, low = blocks(quarter)
    both = dot(table, high)
    z = both[: 2 * WIN] + both[2 * WIN :] + dot(table[: 2 * WIN], low)
    return [(z[:WIN, j * WIN : (j + 1) * WIN], z[WIN:, j * WIN : (j + 1) * WIN]) for j in range(2)]


def probe_step(probe, sums):
    scale = lax.rsqrt(sums[2] + 1.0)
    return [probe[k] + (sums[k] - probe[k] * sums[2]) * scale for k in range(2)]


def sweep_kernel(
    iteration, updates,
    rows_hbm, cols_hbm, counts_hbm, rows_in, cols_in, counts_in, probe_hbm, old_hbm, tables_hbm, strip_hbm,
    amp_hbm, amp_in, out_hbm, sums_out, probe_out,
    rows, cols, counts, rows2, cols2, counts2, tables, split_tables, probe, old_sums, strip, sums, amp, probe_sums,
    small_sem, strip_sem, amp_sem, out_sem,
):
    half = amp.shape[0] // 2
    core = lax.axis_index("pos") % 2
    small = [
        (counts_hbm, counts), (counts_in, counts2), (rows_hbm, rows), (rows_in, rows2), (cols_hbm, cols),
        (cols_in, cols2), (probe_hbm, probe), (tables_hbm, tables),
    ]
    if updates:
        small.append((old_hbm, old_sums))
    copies = [pltpu.make_async_copy(src, dst, small_sem.at[k]) for k, (src, dst) in enumerate(small)]
    copies += [pltpu.make_async_copy(strip_hbm.at[:, k], strip.at[k], strip_sem.at[k]) for k in range(OTILES)]
    for copy in copies:
        copy.start()
    sums_rows = sums.reshape(STILES, ROWS, WIN)
    strip_rows = strip.reshape(OTILES, ROWS, WIN)
    probe_rows = probe_sums.reshape(ROWS // WIN, WIN, WIN)
    for k in range(STILES):
        sums_rows[k] = jnp.zeros((ROWS, WIN), f32)
    for k in range(ROWS // WIN):
        probe_rows[k] = jnp.zeros((WIN, WIN), f32)
    for copy in copies[:2]:
        copy.wait()
    mine = (counts[0, iteration] + 1 - core) // 2
    count = mine + (counts2[0, iteration] + 1 - core) // 2
    amp_copies = []
    for source, live in ((0, mine), (1, count - mine)):
        for k in range(half // GRAIN):
            part, at = pl.ds(k * GRAIN, GRAIN), pl.ds(source * half + k * GRAIN, GRAIN)
            src = amp_in.at[iteration, part] if source else amp_hbm.at[iteration, part, core]
            copy = pltpu.make_async_copy(src, amp.at[at], amp_sem.at[source, k])
            amp_copies.append((live > k * GRAIN, copy))
    for needed, copy in amp_copies:
        pl.when(needed)(copy.start)
    for copy in copies[2:]:
        copy.wait()
    if updates:
        stepped = probe_step(probe, old_sums.reshape(ROWS // WIN, WIN, WIN))
        for k in range(2):
            probe[k] = stepped[k]
    probe_out[...] = probe[...]
    for k in range(2):
        split_tables[k, : 2 * WIN], split_tables[k, 2 * WIN :] = split(tables[k])
    for needed, copy in amp_copies:
        pl.when(needed)(copy.wait)
    lane = lax.broadcasted_iota(jnp.int32, (WIN, WIN), 1)

    def body(k, carry):
        def find(number):
            theirs = number >= mine
            place = jnp.minimum(jnp.where(theirs, number - mine, number), half - 1)
            slot = 2 * place + core
            row = jnp.where(theirs, rows2[iteration, slot], rows[iteration, slot])
            col = jnp.where(theirs, cols2[iteration, slot], cols[iteration, slot])
            first, turn = col // WIN, col % WIN
            second = jnp.minimum(first + 1, COLS - 1)
            return number, jnp.where(theirs, half + place, place), pl.ds(row, WIN), first, second, turn

        def window(found):
            _, _, row, first, second, turn = found
            here = lane >= turn
            q = [
                jnp.where(here, strip_rows[COLS * p + first, row, :], strip_rows[COLS * p + second, row, :])
                for p in range(2)
            ]
            return here, q, [pltpu.roll(probe[p], turn, 1) for p in range(2)]

        def exit_wave(found):
            _, (qr, qi), (pr, pi) = window(found)
            return pr * qr - pi * qi, pr * qi + pi * qr

        def scaled(found, z):
            number, place = found[:2]
            re, im = z
            factor = amp[place] * lax.rsqrt(re * re + im * im + 1.0)
            factor = jnp.where(number < count, factor, 0.0)
            return re * factor, im * factor

        def add(found, g):
            number, _, row, first, second, turn = found
            here, (qr, qi), (pr, pi) = window(found)
            gr, gi = g
            live = (number < count).astype(f32)
            for p, term in enumerate((pr * gr + pi * gi, pr * gi - pi * gr, (pr * pr + pi * pi) * live)):
                sums_rows[COLS * p + first, row, :] += jnp.where(here, term, 0.0)
                sums_rows[COLS * p + second, row, :] += jnp.where(here, 0.0, term)
            back = jnp.where(turn == 0, 0, WIN - turn)
            for p, term in enumerate((qr * gr + qi * gi, qr * gi - qi * gr, (qr * qr + qi * qi) * live)):
                probe_rows[p] += pltpu.roll(term, back, 1)

        pairs = BLOCK // 2
        found, value = [None] * pairs, [None] * pairs
        for step in range(pairs + 6):
            for stage in range(7):
                pair = step - stage
                if not 0 <= pair < pairs:
                    continue
                if stage == 0:
                    found[pair] = [find(k * BLOCK + 2 * pair + j) for j in range(2)]
                    value[pair] = [exit_wave(slot) for slot in found[pair]]
                elif stage in (1, 4):
                    value[pair] = along_columns(value[pair], split_tables[stage // 4])
                elif stage in (2, 5):
                    value[pair] = along_rows(value[pair], split_tables[1 - stage // 4])
                elif stage == 3:
                    value[pair] = [scaled(slot, z) for slot, z in zip(found[pair], value[pair])]
                else:
                    for slot, g in zip(found[pair], value[pair]):
                        add(slot, g)
        return carry

    lax.fori_loop(0, (count + BLOCK - 1) // BLOCK, body, 0)
    outs = [pltpu.make_async_copy(sums.at[k], out_hbm.at[:, k], out_sem.at[k]) for k in range(STILES)]
    outs.append(pltpu.make_async_copy(probe_sums, sums_out, out_sem.at[STILES]))
    for copy in outs:
        copy.start()
    for copy in outs:
        copy.wait()


GRAIN = 4
VMEM_BYTES = 60 * 1024 * 1024
ANY = pl.BlockSpec(memory_space=pl.ANY)
VMEM = pl.BlockSpec(memory_space=pltpu.VMEM)


def dma(*shape):
    return pltpu.SemaphoreType.DMA(shape)


def sweep(iteration, strip, probe, old_sums, offsets, amplitudes, amplitudes_in, tables):
    cap = offsets[0].shape[1]
    updates = old_sums is not None
    return pl.pallas_call(
        functools.partial(sweep_kernel, iteration, updates),
        out_shape=(
            jax.ShapeDtypeStruct((GROUPS, STILES, 8, WIN), f32),
            jax.ShapeDtypeStruct((GROUPS, 8, WIN), f32),
            jax.ShapeDtypeStruct(probe.shape, f32),
        ),
        in_specs=[ANY] * 12,
        out_specs=(ANY, ANY, VMEM),
        scratch_shapes=[pltpu.SMEM(array.shape, jnp.int32) for array in offsets]
        + [
            pltpu.VMEM(tables.shape, f32),
            pltpu.VMEM((2, 4 * WIN, 2 * WIN), jnp.bfloat16),
            pltpu.VMEM(probe.shape, f32),
            pltpu.VMEM((GROUPS, 8, WIN), f32),
            pltpu.VMEM((OTILES, GROUPS, 8, WIN), f32),
            pltpu.VMEM((STILES, GROUPS, 8, WIN), f32),
            pltpu.VMEM((cap, WIN, WIN), f32),
            pltpu.VMEM((GROUPS, 8, WIN), f32),
            dma(10),
            dma(OTILES),
            dma(2, cap // 2 // GRAIN),
            dma(STILES + 1),
        ],
        compiler_params=pltpu.CompilerParams(vmem_limit_bytes=VMEM_BYTES),
        name="sweep",
    )(*offsets, probe, old_sums if updates else probe, tables, strip, amplitudes, amplitudes_in)


class Place:
    def __init__(self):
        pos = lax.axis_index("pos")
        self.tile = lax.axis_index("tile")
        core, y, x = pos % 2, pos // 2 % RING, pos // (2 * RING)
        self.core = core
        self.near, self.far = x + core * (y - x), y + core * (x - y)
        self.near_step, self.far_step = 8 - 6 * core, 2 + 6 * core

    def at(self, near, far):
        return (self.near + near) % RING * self.near_step + (self.far + far) % RING * self.far_step + self.core

    def other_at(self, near, far):
        return (self.far + near) % RING * self.far_step + (self.near + far) % RING * self.near_step + 1 - self.core

    def near_peer(self, k):
        return {"pos": self.at(k, 0)}

    def far_peer(self, k):
        return {"pos": self.at(0, k)}

    def other(self):
        return {"pos": self.other_at(0, 0)}

    def tile_peer(self, k, tiles):
        return {"tile": (self.tile + k) % tiles}


def greet(place, tiles):
    barrier = pltpu.get_barrier_semaphore()
    peers = [place.other()] + [place.near_peer(k) for k in AWAY] + [place.far_peer(k) for k in AWAY]
    peers += [place.tile_peer(k, tiles) for k in range(1, tiles)]
    for peer in peers:
        pl.semaphore_signal(barrier, inc=1, device_id=peer, device_id_type=MESH)
    pl.semaphore_wait(barrier, len(peers))


class Sender:
    def __init__(self, send_sem, recv_sem):
        self.send_sem, self.recv_sem = send_sem, recv_sem
        self.names, self.sent = {}, []

    def copy(self, name, src, dst, device):
        k = self.names.setdefault(name, len(self.names))
        return pltpu.make_async_remote_copy(
            src_ref=src, dst_ref=dst, send_sem=self.send_sem.at[k], recv_sem=self.recv_sem.at[k],
            device_id=device, device_id_type=MESH)

    def send(self, name, src, dst, device):
        copy = self.copy(name, src, dst, device)
        copy.start()
        self.sent.append(copy)

    def arrive(self, name, dst, device):
        self.copy(name, dst, dst, device).wait_recv()

    def finish(self):
        for copy in self.sent:
            copy.wait_send()


class Reduce:
    def __init__(self, place, sender, src, own, core_in, far_in, near_in, load_sem, relay=False):
        self.place, self.sender, self.src, self.own = place, sender, src, own
        self.core_in, self.far_in, self.near_in, self.load_sem = core_in, far_in, near_in, load_sem
        self.loads = {}

    def load(self):
        for far in ALL:
            for near in ALL:
                copy = pltpu.make_async_copy(
                    self.src.at[pl.ds(2 * self.place.at(near, far), 2)], self.own.at[:, near, far],
                    self.load_sem.at[4 * near + far])
                copy.start()
                self.loads[near, far] = copy

    def core_send(self, h):
        for far in ALL:
            for near in ALL:
                self.sender.send(("core", h, near, far), self.src.at[2 * self.place.other_at(near, far) + h],
                                 self.core_in.at[h, near, far], self.place.other())

    def pair(self, h, near, far):
        copy = self.loads.pop((near, far), None)
        if copy is not None:
            copy.wait()
        self.sender.arrive(("core", h, near, far), self.core_in.at[h, near, far], self.place.other())
        self.own[h, near, far] += self.core_in[h, near, far]

    def far_send(self, h, fars=AWAY):
        for far in fars:
            for near in ALL:
                self.pair(h, near, far)
                self.sender.send(("far", h, near, far), self.own.at[h, near, far], self.far_in.at[h, far - 1, near],
                                 self.place.far_peer(far))

    relay_in = None

    def far_first(self, h):
        for near in ALL:
            self.pair(h, near, 2)
            for k, far in enumerate((1, 3)):
                part = pl.ds(k * STILES // 2, STILES // 2)
                self.sender.send(("relay", h, near, far), self.own.at[h, near, 2, part], self.relay_in.at[h, k, near],
                                 self.place.far_peer(far))

    def far_second(self, h):
        for near in ALL:
            for k, far in enumerate((1, 3)):
                self.pair(h, near, far)
                part = pl.ds(k * STILES // 2, STILES // 2)
                at = self.relay_in.at[h, k, near]
                self.sender.arrive(("relay", h, near, far), at, self.place.far_peer(RING - far))
                self.own[h, near, far, part] += at[...]
                self.sender.send(("far", h, near, far), self.own.at[h, near, far], self.far_in.at[h, far - 1, near],
                                 self.place.far_peer(far))

    def line(self, h, near):
        self.pair(h, near, 0)
        total = self.own[h, near, 0]
        for far in (1, 3) if self.relay_in is not None else (1, 3, 2):
            at = self.far_in.at[h, far - 1, near]
            self.sender.arrive(("far", h, near, far), at, self.place.far_peer(RING - far))
            total = total + at[...]
        self.own[h, near, 0] = total

    def near_send(self, h):
        for near in AWAY:
            self.line(h, near)
            self.sender.send(("near", h, near), self.own.at[h, near, 0], self.near_in.at[h, near - 1],
                             self.place.near_peer(near))

    def total(self, h):
        self.line(h, 0)
        total = self.own[h, 0, 0]
        for near in (1, 3, 2):
            at = self.near_in.at[h, near - 1]
            self.sender.arrive(("near", h, near), at, self.place.near_peer(RING - near))
            total = total + at[...]
        return total


class Gather:
    def __init__(self, place, sender, buf, name="o"):
        self.place, self.sender, self.buf, self.name = place, sender, buf, name

    def at(self, h, near, far):
        return self.buf.at[2 * self.place.at(near, far) + h]

    def spread(self, h, near):
        for far in (1, 3) if near in self.relays else AWAY:
            self.sender.send((self.name, "far", h, near, far), self.at(h, near, 0), self.at(h, near, 0), self.place.far_peer(far))

    def to_core(self, h, near, far):
        self.sender.send((self.name, "core", h, near, far), self.at(h, near, far), self.at(h, near, far), self.place.other())

    def start(self, h):
        for near in AWAY:
            self.sender.send((self.name, "near", h, near), self.at(h, 0, 0), self.at(h, 0, 0), self.place.near_peer(near))
        self.spread(h, 0)
        self.to_core(h, 0, 0)

    relays = ()

    def half(self, h, near, far, k):
        return self.buf.at[2 * self.place.at(near, far) + h, pl.ds(4 * k, 4)]

    def relay(self, h, near):
        for k, far in enumerate((1, 3)):
            back = RING - far
            self.sender.arrive((self.name, "far", h, near, far), self.at(h, near, back), self.place.far_peer(back))
            at = self.half(h, near, back, k)
            self.sender.send((self.name, "relay", h, near, far), at, at, self.place.far_peer(far))
            self.to_core(h, near, back)

    def relayed(self, h, near):
        for k, far in enumerate((1, 3)):
            self.sender.arrive((self.name, "relay", h, near, far), self.half(h, near, 2, k), self.place.far_peer(RING - far))
        self.to_core(h, near, 2)

    def middle(self, h):
        for near in (1, 3, 2):
            self.sender.arrive((self.name, "near", h, RING - near), self.at(h, near, 0), self.place.near_peer(near))
            self.spread(h, near)
        for near in (1, 3, 2):
            self.to_core(h, near, 0)

    def end(self, h, nears=(0, 1, 3, 2)):
        for near in self.relays:
            self.relay(h, near)
        for near in nears:
            if near in self.relays:
                continue
            for far in (1, 3, 2):
                self.sender.arrive((self.name, "far", h, near, RING - far), self.at(h, near, far), self.place.far_peer(far))
                self.to_core(h, near, far)

    def done(self, h):
        for near in self.relays:
            self.relayed(h, near)
        for near in range(RING):
            for far in range(RING):
                at = self.buf.at[2 * self.place.other_at(near, far) + h]
                self.sender.arrive((self.name, "core", h, near, far), at, self.place.other())


class ProbeSum:
    def __init__(self, place, sender, src, tiles, own, core_in, table, far_in, line, near_in, seen, all_, other_all, load_sem):
        self.place, self.sender, self.src, self.tiles = place, sender, src, tiles
        self.own, self.core_in, self.table, self.far_in, self.line = own, core_in, table, far_in, line
        self.near_in, self.seen, self.all, self.other_all, self.load_sem = near_in, seen, all_, other_all, load_sem

    def load(self):
        self.copy = pltpu.make_async_copy(self.src.at[:, :, self.place.core], self.own, self.load_sem)
        self.copy.start()

    def core(self):
        self.sender.send("pcore", self.src.at[:, :, 1 - self.place.core], self.core_in, self.place.other())

    def far(self):
        place = self.place
        self.copy.wait()
        self.sender.arrive("pcore", self.core_in, place.other())
        for x in range(RING):
            for y in range(RING):
                near, far = x + place.core * (y - x), y + place.core * (x - y)
                self.table[near, far] = self.own[x, y] + self.core_in[x, y]
        for k in AWAY:
            src = self.table.at[:, (place.far + k) % RING]
            self.sender.send(("pfar", k), src, self.far_in.at[k - 1], place.far_peer(k))

    def near(self):
        place = self.place
        total = self.table[:, place.far]
        for k in (1, 3, 2):
            self.sender.arrive(("pfar", k), self.far_in.at[k - 1], place.far_peer(RING - k))
            total = total + self.far_in[k - 1]
        self.line[...] = total
        for k in AWAY:
            src = self.line.at[(place.near + k) % RING]
            self.sender.send(("pnear", k), src, self.near_in.at[k - 1], place.near_peer(k))

    def across(self):
        place = self.place
        total = self.line[place.near]
        for k in (1, 3, 2):
            self.sender.arrive(("pnear", k), self.near_in.at[k - 1], place.near_peer(RING - k))
            total = total + self.near_in[k - 1]
        self.seen[place.tile] = total
        for k in range(1, self.tiles):
            at = self.seen.at[place.tile]
            self.sender.send(("ptile", k), at, at, place.tile_peer(k, self.tiles))

    def back_near(self):
        place = self.place
        for k in range(1, self.tiles):
            source = (place.tile + self.tiles - k) % self.tiles
            self.sender.arrive(("ptile", k), self.seen.at[source], {"tile": source})
        total = self.seen[0]
        for k in range(1, self.tiles):
            total = total + self.seen[k]
        self.all[place.near, place.far] = total
        at = self.all.at[place.near, place.far]
        for k in AWAY:
            self.sender.send(("pback", k), at, at, place.near_peer(k))

    def back_far(self):
        place = self.place
        for k in (1, 3, 2):
            at = self.all.at[(place.near + RING - k) % RING, place.far]
            self.sender.arrive(("pback", k), at, place.near_peer(RING - k))
        at = self.all.at[:, place.far]
        for k in AWAY:
            self.sender.send(("pout", k), at, at, place.far_peer(k))

    def back_core(self):
        place = self.place
        for k in (1, 3, 2):
            at = self.all.at[:, (place.far + RING - k) % RING]
            self.sender.arrive(("pout", k), at, place.far_peer(RING - k))
        self.sender.send("pother", self.all, self.other_all, place.other())

    def finish(self, out):
        core = self.place.core
        self.sender.arrive("pother", self.other_all, self.place.other())
        for near in range(RING):
            for far in range(RING):
                x, y = near + core * (far - near), far + core * (near - far)
                out[x, y, core] = self.all[near, far]
                out[y, x, 1 - core] = self.other_all[near, far]


def gather_kernel(
    object_ref, amp_hbm, rows_hbm, cols_hbm, counts_hbm, out_hbm, amp_in, rows_in, cols_in, counts_in,
    mine, send_sem, recv_sem, copy_sem,
):
    place = Place()
    for g in range(2):
        for p in range(2):
            for b in range(COLS):
                mine[g, COLS * p + b] = object_ref[p, 8 * g : 8 * g + 8, WIN * b : WIN * b + WIN]
    copy = pltpu.make_async_copy(mine, out_hbm.at[pl.ds(2 * place.at(0, 0), 2)], copy_sem)
    copy.start()
    greet(place, 1)
    copy.wait()
    sender = Sender(send_sem, recv_sem)
    strip = Gather(place, sender, out_hbm)
    strip.start(0)
    strip.start(1)
    other = place.other()
    moves = [(counts_hbm, counts_in), (rows_hbm, rows_in), (cols_hbm, cols_in)]
    moves += [(amp_hbm.at[k, :, 1 - place.core], amp_in.at[k]) for k in range(amp_in.shape[0])]
    for k, (src, dst) in enumerate(moves):
        sender.send(("move", k), src, dst, other)
    for h in range(2):
        strip.middle(h)
    for h in range(2):
        strip.end(h)
    for h in range(2):
        strip.done(h)
    for k, (_, dst) in enumerate(moves):
        sender.arrive(("move", k), dst, other)
    sender.finish()


def exchange_kernel(
    tiles, last, sums_hbm, probe_src, strip_hbm, *refs,
):
    if last:
        probe_ref, object_out, probe_out = refs[:3]
        refs = refs[3:]
    else:
        out_hbm, sums_out = refs[:2]
        refs = refs[2:]
    (old, own, core_in, far_in, near_in, relay_in, mine,
     p_own, p_core, p_table, p_far, p_line, p_near, p_seen, p_all, p_other, p_out,
     load_sem, copy_sem, send_sem, recv_sem, send_sem2, recv_sem2, send_sem3, recv_sem3) = refs
    place = Place()
    here = pl.ds(2 * place.at(0, 0), 2)
    load = pltpu.make_async_copy(strip_hbm.at[here], old, copy_sem.at[0])
    load.start()
    first, second, third = Sender(send_sem, recv_sem), Sender(send_sem2, recv_sem2), Sender(send_sem3, recv_sem3)
    sums = Reduce(place, first, sums_hbm, own, core_in, far_in, near_in, load_sem)
    sums.relay_in = relay_in
    probe = ProbeSum(
        place, third, probe_src, tiles, p_own, p_core, p_table, p_far, p_line, p_near, p_seen, p_all, p_other,
        copy_sem.at[3],
    )
    probe.load()
    sums.load()
    greet(place, tiles)
    probe.core()
    sums.core_send(0)
    sums.core_send(1)
    probe.far()
    sums.far_first(0)
    sums.far_first(1)
    probe.near()
    sums.far_second(0)
    probe.across()
    sums.far_second(1)
    sums.near_send(0)
    probe.back_near()
    sums.near_send(1)
    strip = None if last else Gather(place, second, out_hbm)

    def step(h):
        total = sums.total(h)
        if h == 0:
            load.wait()
        for b in range(COLS):
            scale = 1.0 / (total[2 * COLS + b] + 1.0)
            for p in range(2):
                tile = (old[h, COLS * p + b] + total[COLS * p + b]) * scale
                if last:
                    object_out[p, 8 * h : 8 * h + 8, WIN * b : WIN * b + WIN] = tile
                else:
                    mine[h, COLS * p + b] = tile
        if not last:
            copy = pltpu.make_async_copy(mine.at[h], strip.at(h, 0, 0), copy_sem.at[1 + h])
            copy.start()
            copy.wait()
            strip.start(h)

    probe.back_far()
    step(0)
    step(1)
    probe.back_core()
    if last:
        probe.finish(p_out)
        stepped = probe_step(probe_ref, p_out.reshape(ROWS // WIN, WIN, WIN))
        for k in range(2):
            probe_out[k] = stepped[k]
    else:
        for h in range(2):
            strip.middle(h)
        probe.finish(sums_out)
        for h in range(2):
            strip.end(h)
        for h in range(2):
            strip.done(h)
    for sender in (first, second, third):
        sender.finish()


def params(collective_id):
    return pltpu.CompilerParams(collective_id=collective_id, has_side_effects=True, vmem_limit_bytes=VMEM_BYTES)


GATHER_COPIES, REDUCE_COPIES = 62, 70


def gather_object(object_field, amplitudes, offsets):
    copies = GATHER_COPIES + 3 + amplitudes.shape[0]
    halves = amplitudes.shape[:2] + amplitudes.shape[3:]
    return pl.pallas_call(
        gather_kernel,
        out_shape=[jax.ShapeDtypeStruct((GROUPS, OTILES, 8, WIN), f32), jax.ShapeDtypeStruct(halves, f32)]
        + [jax.ShapeDtypeStruct(array.shape, jnp.int32) for array in offsets],
        in_specs=[VMEM] + [ANY] * 4,
        out_specs=[ANY] * 5,
        scratch_shapes=[pltpu.VMEM((2, OTILES, 8, WIN), f32), dma(copies), dma(copies), pltpu.SemaphoreType.DMA],
        compiler_params=params(0),
        name="gather_object",
    )(object_field, amplitudes, *offsets)


def exchange(sums, probe_sums, strip, probe, object_shape):
    tiles = lax.axis_size("tile")
    is_last = probe is not None
    by_device = (RING, RING, 2, 2, 8, WIN)
    if is_last:
        out_shape = (jax.ShapeDtypeStruct(object_shape, f32), jax.ShapeDtypeStruct(probe.shape, f32))
        out_specs = (VMEM, VMEM)
    else:
        out_shape = (jax.ShapeDtypeStruct(strip.shape, f32), jax.ShapeDtypeStruct(by_device, f32))
        out_specs = (ANY, VMEM)
    group, pair = (STILES, 8, WIN), (2, 8, WIN)
    buffers = [
        (2, OTILES, 8, WIN), (2, RING, RING) + group, (2, RING, RING) + group, (2, 3, RING) + group, (2, 3) + group,
        (2, 2, RING, STILES // 2, 8, WIN), (2, OTILES, 8, WIN),
        (RING, RING) + pair, (RING, RING) + pair, (RING, RING) + pair, (3, RING) + pair, (RING,) + pair, (3,) + pair,
        (tiles,) + pair, (RING, RING) + pair, (RING, RING) + pair, by_device,
    ]
    return pl.pallas_call(
        functools.partial(exchange_kernel, tiles, is_last),
        out_shape=out_shape,
        in_specs=[ANY, ANY, ANY] + ([VMEM] if is_last else []),
        out_specs=out_specs,
        scratch_shapes=[pltpu.VMEM(shape, f32) for shape in buffers]
        + [dma(RING * RING), dma(4)]
        + [dma(REDUCE_COPIES)] * 2 + [dma(GATHER_COPIES)] * 2 + [dma(14 + tiles - 1)] * 2,
        compiler_params=params(2 if is_last else 1),
        name="exchange_last" if is_last else "exchange_middle",
    )(sums, probe_sums.reshape(by_device), strip, *([probe] if is_last else []))


def per_device(object_field, illumination, row_offsets, col_offsets, counts, amplitudes):
    tables = jnp.asarray(transform_tables())
    offsets = [row_offsets, col_offsets, counts.T]
    iterations, cap = row_offsets.shape
    amplitudes = amplitudes.reshape(iterations, cap // 2, 2, WIN, WIN)
    strip, amplitudes_in, *offsets_in = gather_object(object_field, amplitudes, offsets)
    probe, old_sums = illumination, None
    for iteration in range(iterations):
        sums, probe_sums, probe = sweep(
            iteration, strip, probe, old_sums, offsets + offsets_in, amplitudes, amplitudes_in, tables
        )
        if iteration + 1 < iterations:
            strip, old_sums = exchange(sums, probe_sums, strip, None, None)
            old_sums = old_sums.reshape(GROUPS, 8, WIN)
    return exchange(sums, probe_sums, strip, probe, object_field.shape)


def solution(mesh):
    return jax.shard_map(
        per_device,
        mesh=mesh,
        in_specs=(
            P(None, "pos", "tile"),
            P(),
            P(None, ("tile", "pos")),
            P(None, ("tile", "pos")),
            P(None, ("tile", "pos")),
            P(None, ("tile", "pos"), None, None),
        ),
        out_specs=(P(None, "pos", "tile"), P()),
        check_vma=False,
    )
```

time: 1660 us -> 127 us (0.08); the launches traced: 1630 us -> 126 us
  waiting for transfers between devices: 1360 us -> 0 us
  Pallas kernels: 0 us -> 123 us
  local copies, waits for them, and re-layouts: 98.4 us -> 3.04 us
  loops' own time: 81.5 us -> 0 us
  other arithmetic: 36.1 us -> 0 us
  matrix products: 34.5 us -> 0 us
    psum x2 -> x0, waiting for transfers between devices: 797 us -> none  [per_device(): lax.psum((probe_local[:2], probe_local[2]), ('tile', 'pos'))]
    reduce_scatter x2 -> x0, waiting for transfers between devices: 466 us -> none  [per_device(): owned = lax.psum_scatter(totals, 'pos', scatter_dimension=1, tiled=True)]
    pallas_call x0 -> x5, Pallas kernels: none -> 123 us  [the longest x2 80.8 us: exchange(): pl.pallas_call(functools.partial(exchange_kernel, tiles, is_last), out_sh...]
    all_gather x2 -> x0, waiting for transfers between devices: 97.8 us -> none  [fetch_strip(): return lax.all_gather(object_shard, 'pos', axis=1, tiled=True)]
    another operation x10 -> x0, loops' own time: 81.5 us -> none  [the longest x8 60.9 us: advance(): return lax.cond(jnp.any(block_alive > 0), busy, unchanged, carry)]
    dynamic_update_slice x16 -> x0, local copies, waits for them, and re-layouts: 64.6 us -> none  [busy(): lax.dynamic_update_slice(totals, current + object_terms[slot_number], whe...]
    dot_general x32 -> x0, matrix products: 34.5 us -> none  [the longest x4 6.1 us: transform(): jnp.einsum('bij,jk->bik', left_imag, cosine, precision=exact_mode)]
    add x20 -> x0, other arithmetic: 23.6 us -> none  [the longest x16 18.2 us: busy(): current + object_terms[slot_number]]
  transfers between devices with their start and end apart: 6 -> 0, of which waited for: 6 -> 0; matrix products, arithmetic and copies ran while one was open for 1% -> 0% of each run, Pallas kernels for 0% -> 0%
where the time goes in v2:
time: 127 us; the launch traced here: 126 us
  Pallas kernels  123 us (97%)
  local copies, waits for them, and re-layouts  3.04 us (2%)
    pallas_call x2, Pallas kernels, exchange(): pl.pallas_call(functools.partial(exchange_kernel, tiles, is_last), out_sh...  80.8 us
    pallas_call x2, Pallas kernels, sweep(): pl.pallas_call(functools.partial(sweep_kernel, iteration, updates), out_s...  21.2 us
    pallas_call x1, Pallas kernels, gather_object(): pl.pallas_call(gather_kernel, out_shape=[jax.ShapeDtypeStruct((GROUPS, OT...  20.6 us
    unnamed x2, local copies, waits for them, and re-layouts  3.04 us

profile of v2, /device:TPU:1, one launch (start us, length us, event | category | flops | bytes accessed | tf_op | source)
XLA Modules:
  0.0 126.3 jit_solution(15701204040542131971)
XLA Ops:
  0.6 20.6 %gather_object.1 = (f32[64,8,8,128]{3,2,1,0:T(8,128)}, f32[2,16,128,128]{3,2,1,0:T(8,128)}, s32[2,32]{1,0:T(2,128)}, s32[2,32]{1,0:T(2,128)}, s32[1,2]{1,0:T(1,128)}) custom-call(f32[2,16,512]{2,1,0:T(8,128)} %object_ref.1, f32[2,16,2,128,128]{4,3,2,1,0:T(8,128)} %bitcast.5, s32[2,32]{1,0:T(2,128)} %rows_hbm.5, s32[2,32]{1,0:T(2,128)} %cols_hbm.5, ...), custom_call_target="tpu_custom_call" | custom-call | tf_op jit(solution)/shard_map/gather_object/pallas_call | solution.py:647
  21.2 10.6 %sweep.2 = (f32[64,12,8,128]{3,2,1,0:T(8,128)}, f32[64,8,128]{2,1,0:T(8,128)}, f32[2,128,128]{2,1,0:T(8,128)}) custom-call(s32[2,32]{1,0:T(2,128)} %rows_hbm.5, s32[2,32]{1,0:T(2,128)} %cols_hbm.5, s32[1,2]{1,0:T(1,128)} %bitcast.12, s32[2,32]{1,0:T(2,128)} %get-tuple-element.15.rows_in, s32[2,32]{1,0:T(2,128)} %get-tuple-element.16.cols_in, ...), custom_call_target="tpu_custom_call" | custom-call | tf_op jit(solution)/shard_map/sweep/pallas_call | solution.py:203
  31.8 46.2 %exchange_middle.1 = (f32[64,8,8,128]{3,2,1,0:T(8,128)}, f32[4,4,2,2,8,128]{5,4,3,2,1,0:T(8,128)}) custom-call(f32[64,12,8,128]{3,2,1,0:T(8,128)} %get-tuple-element.21.sums_hbm, f32[4,4,2,2,8,128]{5,4,3,2,1,0:T(8,128)} %bitcast.10, f32[64,8,8,128]{3,2,1,0:T(8,128)} %get-tuple-element.18.strip_hbm), custom_call_target="tpu_custom_call" | custom-call | tf_op jit(solution)/shard_map/exchange_middle/pallas_call | solution.py:676
  78.0 10.6 %sweep.3 = (f32[64,12,8,128]{3,2,1,0:T(8,128)}, f32[64,8,128]{2,1,0:T(8,128)}, f32[2,128,128]{2,1,0:T(8,128)}) custom-call(s32[2,32]{1,0:T(2,128)} %rows_hbm.5, s32[2,32]{1,0:T(2,128)} %cols_hbm.5, s32[1,2]{1,0:T(1,128)} %bitcast.13, s32[2,32]{1,0:T(2,128)} %get-tuple-element.15.rows_in, s32[2,32]{1,0:T(2,128)} %get-tuple-element.16.cols_in, ...), custom_call_target="tpu_custom_call" | custom-call | tf_op jit(solution)/shard_map/sweep/pallas_call | solution.py:203
  88.6 34.6 %exchange_last.1 = (f32[2,16,512]{2,1,0:T(8,128)}, f32[2,128,128]{2,1,0:T(8,128)}) custom-call(f32[64,12,8,128]{3,2,1,0:T(8,128)} %get-tuple-element.25.sums_hbm, f32[4,4,2,2,8,128]{5,4,3,2,1,0:T(8,128)} %bitcast.9, f32[64,8,8,128]{3,2,1,0:T(8,128)} %get-tuple-element.24.strip_hbm, f32[2,128,128]{2,1,0:T(8,128)} %get-tuple-element.27.refs_0_), custom_call_target="tpu_custom_call" | custom-call | tf_op jit(solution)/shard_map/exchange_last/pallas_call | solution.py:676
  123.2 1.5 %copy.11 = f32[2,16,512]{2,1,0:T(8,128)} copy(f32[2,16,512]{2,1,0:T(8,128)} %get-tuple-element.30) | data formatting | bytes 131072
  124.7 1.6 %copy.12 = f32[2,128,128]{2,1,0:T(8,128)} copy(f32[2,128,128]{2,1,0:T(8,128)} %get-tuple-element.31) | data formatting | bytes 262144

commit v3 on v2

--- a/solution.py
+++ b/solution.py
@@ -14,6 +14,7 @@
 ROWS = 512
 GROUPS = ROWS // 8
 COLS = ROWS // WIN
+PTILES = 3 * WIN // 8
 OTILES, STILES = 2 * COLS, 3 * COLS
 BLOCK = 8
 RING = 4
@@ -83,10 +84,10 @@
         copy.start()
     sums_rows = sums.reshape(STILES, ROWS, WIN)
     strip_rows = strip.reshape(OTILES, ROWS, WIN)
-    probe_rows = probe_sums.reshape(ROWS // WIN, WIN, WIN)
+    probe_rows = probe_sums.reshape(3, WIN, WIN)
     for k in range(STILES):
         sums_rows[k] = jnp.zeros((ROWS, WIN), f32)
-    for k in range(ROWS // WIN):
+    for k in range(3):
         probe_rows[k] = jnp.zeros((WIN, WIN), f32)
     for copy in copies[:2]:
         copy.wait()
@@ -104,7 +105,7 @@
     for copy in copies[2:]:
         copy.wait()
     if updates:
-        stepped = probe_step(probe, old_sums.reshape(ROWS // WIN, WIN, WIN))
+        stepped = probe_step(probe, old_sums.reshape(3, WIN, WIN))
         for k in range(2):
             probe[k] = stepped[k]
     probe_out[...] = probe[...]
@@ -114,7 +115,7 @@
         pl.when(needed)(copy.wait)
     lane = lax.broadcasted_iota(jnp.int32, (WIN, WIN), 1)
 
-    def body(k, carry):
+    def work(begin, size):
         def find(number):
             theirs = number >= mine
             place = jnp.minimum(jnp.where(theirs, number - mine, number), half - 1)
@@ -157,7 +158,7 @@
             for p, term in enumerate((qr * gr + qi * gi, qr * gi - qi * gr, (qr * qr + qi * qi) * live)):
                 probe_rows[p] += pltpu.roll(term, back, 1)
 
-        pairs = BLOCK // 2
+        pairs = size // 2
         found, value = [None] * pairs, [None] * pairs
         for step in range(pairs + 6):
             for stage in range(7):
@@ -165,7 +166,7 @@
                 if not 0 <= pair < pairs:
                     continue
                 if stage == 0:
-                    found[pair] = [find(k * BLOCK + 2 * pair + j) for j in range(2)]
+                    found[pair] = [find(begin + 2 * pair + j) for j in range(2)]
                     value[pair] = [exit_wave(slot) for slot in found[pair]]
                 elif stage in (1, 4):
                     value[pair] = along_columns(value[pair], split_tables[stage // 4])
@@ -176,9 +177,14 @@
                 else:
                     for slot, g in zip(found[pair], value[pair]):
                         add(slot, g)
+
+    def body(k, carry):
+        work(k * BLOCK, BLOCK)
         return carry
 
-    lax.fori_loop(0, (count + BLOCK - 1) // BLOCK, body, 0)
+    whole = (count + BLOCK // 2 - 1) // BLOCK
+    lax.fori_loop(0, whole, body, 0)
+    pl.when(count > whole * BLOCK)(lambda: work(whole * BLOCK, BLOCK // 2))
     outs = [pltpu.make_async_copy(sums.at[k], out_hbm.at[:, k], out_sem.at[k]) for k in range(STILES)]
     outs.append(pltpu.make_async_copy(probe_sums, sums_out, out_sem.at[STILES]))
     for copy in outs:
@@ -188,7 +194,7 @@
 
 
 GRAIN = 4
-VMEM_BYTES = 60 * 1024 * 1024
+VMEM_BYTES = 20 * 1024 * 1024
 ANY = pl.BlockSpec(memory_space=pl.ANY)
 VMEM = pl.BlockSpec(memory_space=pltpu.VMEM)
 
@@ -204,7 +210,7 @@
         functools.partial(sweep_kernel, iteration, updates),
         out_shape=(
             jax.ShapeDtypeStruct((GROUPS, STILES, 8, WIN), f32),
-            jax.ShapeDtypeStruct((GROUPS, 8, WIN), f32),
+            jax.ShapeDtypeStruct((PTILES, 8, WIN), f32),
             jax.ShapeDtypeStruct(probe.shape, f32),
         ),
         in_specs=[ANY] * 12,
@@ -214,11 +220,11 @@
             pltpu.VMEM(tables.shape, f32),
             pltpu.VMEM((2, 4 * WIN, 2 * WIN), jnp.bfloat16),
             pltpu.VMEM(probe.shape, f32),
-            pltpu.VMEM((GROUPS, 8, WIN), f32),
+            pltpu.VMEM((PTILES, 8, WIN), f32),
             pltpu.VMEM((OTILES, GROUPS, 8, WIN), f32),
             pltpu.VMEM((STILES, GROUPS, 8, WIN), f32),
             pltpu.VMEM((cap, WIN, WIN), f32),
-            pltpu.VMEM((GROUPS, 8, WIN), f32),
+            pltpu.VMEM((PTILES, 8, WIN), f32),
             dma(10),
             dma(OTILES),
             dma(2, cap // 2 // GRAIN),
@@ -234,7 +240,7 @@
         pos = lax.axis_index("pos")
         self.tile = lax.axis_index("tile")
         core, y, x = pos % 2, pos // 2 % RING, pos // (2 * RING)
-        self.core = core
+        self.core, self.x, self.y = core, x, y
         self.near, self.far = x + core * (y - x), y + core * (x - y)
         self.near_step, self.far_step = 8 - 6 * core, 2 + 6 * core
 
@@ -243,6 +249,12 @@
 
     def other_at(self, near, far):
         return (self.far + near) % RING * self.far_step + (self.near + far) % RING * self.near_step + 1 - self.core
+
+    def x_peer(self, k):
+        return {"pos": (self.x + k) % RING * 8 + self.y * 2 + self.core}
+
+    def y_peer(self, k):
+        return {"pos": self.x * 8 + (self.y + k) % RING * 2 + self.core}
 
     def near_peer(self, k):
         return {"pos": self.at(k, 0)}
@@ -436,96 +448,85 @@
 
 
 class ProbeSum:
-    def __init__(self, place, sender, src, tiles, own, core_in, table, far_in, line, near_in, seen, all_, other_all, load_sem):
-        self.place, self.sender, self.src, self.tiles = place, sender, src, tiles
-        self.own, self.core_in, self.table, self.far_in, self.line = own, core_in, table, far_in, line
-        self.near_in, self.seen, self.all, self.other_all, self.load_sem = near_in, seen, all_, other_all, load_sem
+    def __init__(self, place, sender, src, tiles, own, core_in, tile_in, x_in, y_in, total, load_sem):
+        self.place, self.sender, self.src, self.tiles, self.own, self.core_in = place, sender, src, tiles, own, core_in
+        self.tile_in, self.x_in, self.y_in, self.total, self.load_sem = tile_in, x_in, y_in, total, load_sem
+        self.half = PTILES // 2
+        self.part = self.half // tiles
+
+    def tiles_of(self, core):
+        return pl.ds(core * self.half, self.half)
 
     def load(self):
-        self.copy = pltpu.make_async_copy(self.src.at[:, :, self.place.core], self.own, self.load_sem)
+        self.copy = pltpu.make_async_copy(self.src.at[self.tiles_of(self.place.core)], self.own, self.load_sem)
         self.copy.start()
 
     def core(self):
-        self.sender.send("pcore", self.src.at[:, :, 1 - self.place.core], self.core_in, self.place.other())
-
-    def far(self):
+        self.sender.send("core", self.src.at[self.tiles_of(1 - self.place.core)], self.core_in, self.place.other())
+
+    def across(self):
         place = self.place
         self.copy.wait()
-        self.sender.arrive("pcore", self.core_in, place.other())
-        for x in range(RING):
-            for y in range(RING):
-                near, far = x + place.core * (y - x), y + place.core * (x - y)
-                self.table[near, far] = self.own[x, y] + self.core_in[x, y]
+        self.sender.arrive("core", self.core_in, place.other())
+        self.own[...] += self.core_in[...]
+        for k in range(1, self.tiles):
+            src = self.own.at[pl.ds((place.tile + k) % self.tiles * self.part, self.part)]
+            self.sender.send(("tile", k), src, self.tile_in.at[k - 1], place.tile_peer(k, self.tiles))
+
+    def spread(self, name, buf, at, peer):
         for k in AWAY:
-            src = self.table.at[:, (place.far + k) % RING]
-            self.sender.send(("pfar", k), src, self.far_in.at[k - 1], place.far_peer(k))
-
-    def near(self):
+            self.sender.send((name, k), buf.at[at], buf.at[at], peer(k))
+
+    def collect(self, name, buf, at, peer):
+        for k in (1, 3, 2):
+            self.sender.arrive((name, k), buf.at[(at + RING - k) % RING], peer(RING - k))
+        return (buf[0] + buf[1]) + (buf[2] + buf[3])
+
+    def along_x(self):
         place = self.place
-        total = self.table[:, place.far]
-        for k in (1, 3, 2):
-            self.sender.arrive(("pfar", k), self.far_in.at[k - 1], place.far_peer(RING - k))
-            total = total + self.far_in[k - 1]
-        self.line[...] = total
-        for k in AWAY:
-            src = self.line.at[(place.near + k) % RING]
-            self.sender.send(("pnear", k), src, self.near_in.at[k - 1], place.near_peer(k))
-
-    def across(self):
+        total = self.own[pl.ds(place.tile * self.part, self.part)]
+        for k in range(1, self.tiles):
+            self.sender.arrive(("tile", k), self.tile_in.at[k - 1], place.tile_peer(self.tiles - k, self.tiles))
+            total = total + self.tile_in[k - 1]
+        self.x_in[place.x] = total
+        self.spread("x", self.x_in, place.x, place.x_peer)
+
+    def along_y(self):
         place = self.place
-        total = self.line[place.near]
-        for k in (1, 3, 2):
-            self.sender.arrive(("pnear", k), self.near_in.at[k - 1], place.near_peer(RING - k))
-            total = total + self.near_in[k - 1]
-        self.seen[place.tile] = total
+        self.y_in[place.y] = self.collect("x", self.x_in, place.x, place.x_peer)
+        self.spread("y", self.y_in, place.y, place.y_peer)
+
+    def share(self, tile):
+        return self.total.at[pl.ds(self.place.core * self.half + tile * self.part, self.part)]
+
+    def back(self):
+        place = self.place
+        at = self.share(place.tile)
+        at[...] = self.collect("y", self.y_in, place.y, place.y_peer)
         for k in range(1, self.tiles):
-            at = self.seen.at[place.tile]
-            self.sender.send(("ptile", k), at, at, place.tile_peer(k, self.tiles))
-
-    def back_near(self):
+            self.sender.send(("back", k), at, at, place.tile_peer(k, self.tiles))
+
+    def back_core(self):
         place = self.place
         for k in range(1, self.tiles):
             source = (place.tile + self.tiles - k) % self.tiles
-            self.sender.arrive(("ptile", k), self.seen.at[source], {"tile": source})
-        total = self.seen[0]
-        for k in range(1, self.tiles):
-            total = total + self.seen[k]
-        self.all[place.near, place.far] = total
-        at = self.all.at[place.near, place.far]
-        for k in AWAY:
-            self.sender.send(("pback", k), at, at, place.near_peer(k))
-
-    def back_far(self):
-        place = self.place
-        for k in (1, 3, 2):
-            at = self.all.at[(place.near + RING - k) % RING, place.far]
-            self.sender.arrive(("pback", k), at, place.near_peer(RING - k))
-        at = self.all.at[:, place.far]
-        for k in AWAY:
-            self.sender.send(("pout", k), at, at, place.far_peer(k))
-
-    def back_core(self):
-        place = self.place
-        for k in (1, 3, 2):
-            at = self.all.at[:, (place.far + RING - k) % RING]
-            self.sender.arrive(("pout", k), at, place.far_peer(RING - k))
-        self.sender.send("pother", self.all, self.other_all, place.other())
-
-    def finish(self, out):
-        core = self.place.core
-        self.sender.arrive("pother", self.other_all, self.place.other())
-        for near in range(RING):
-            for far in range(RING):
-                x, y = near + core * (far - near), far + core * (near - far)
-                out[x, y, core] = self.all[near, far]
-                out[y, x, 1 - core] = self.other_all[near, far]
+            self.sender.arrive(("back", k), self.share(source), {"tile": source})
+        at = self.total.at[self.tiles_of(place.core)]
+        self.sender.send("other", at, at, place.other())
+
+    def finish(self):
+        self.sender.arrive("other", self.total.at[self.tiles_of(1 - self.place.core)], self.place.other())
+        return self.total
 
 
 def gather_kernel(
-    object_ref, amp_hbm, rows_hbm, cols_hbm, counts_hbm, out_hbm, amp_in, rows_in, cols_in, counts_in,
-    mine, send_sem, recv_sem, copy_sem,
+    object_hbm, amp_hbm, rows_hbm, cols_hbm, counts_hbm, out_hbm, amp_in, rows_in, cols_in, counts_in,
+    object_ref, mine, send_sem, recv_sem, copy_sem,
 ):
     place = Place()
+    copy = pltpu.make_async_copy(object_hbm, object_ref, copy_sem)
+    copy.start()
+    copy.wait()
     for g in range(2):
         for p in range(2):
             for b in range(COLS):
@@ -564,7 +565,7 @@
         out_hbm, sums_out = refs[:2]
         refs = refs[2:]
     (old, own, core_in, far_in, near_in, relay_in, mine,
-     p_own, p_core, p_table, p_far, p_line, p_near, p_seen, p_all, p_other, p_out,
+     p_own, p_core, p_tile, p_x, p_y, p_total,
      load_sem, copy_sem, send_sem, recv_sem, send_sem2, recv_sem2, send_sem3, recv_sem3) = refs
     place = Place()
     here = pl.ds(2 * place.at(0, 0), 2)
@@ -574,8 +575,7 @@
     sums = Reduce(place, first, sums_hbm, own, core_in, far_in, near_in, load_sem)
     sums.relay_in = relay_in
     probe = ProbeSum(
-        place, third, probe_src, tiles, p_own, p_core, p_table, p_far, p_line, p_near, p_seen, p_all, p_other,
-        copy_sem.at[3],
+        place, third, probe_src, tiles, p_own, p_core, p_tile, p_x, p_y, p_total, copy_sem.at[3]
     )
     probe.load()
     sums.load()
@@ -583,15 +583,14 @@
     probe.core()
     sums.core_send(0)
     sums.core_send(1)
-    probe.far()
     sums.far_first(0)
+    probe.across()
     sums.far_first(1)
-    probe.near()
     sums.far_second(0)
-    probe.across()
+    probe.along_x()
     sums.far_second(1)
     sums.near_send(0)
-    probe.back_near()
+    probe.along_y()
     sums.near_send(1)
     strip = None if last else Gather(place, second, out_hbm)
 
@@ -613,19 +612,18 @@
             copy.wait()
             strip.start(h)
 
-    probe.back_far()
+    probe.back()
     step(0)
     step(1)
     probe.back_core()
     if last:
-        probe.finish(p_out)
-        stepped = probe_step(probe_ref, p_out.reshape(ROWS // WIN, WIN, WIN))
+        stepped = probe_step(probe_ref, probe.finish().reshape(3, WIN, WIN))
         for k in range(2):
             probe_out[k] = stepped[k]
     else:
         for h in range(2):
             strip.middle(h)
-        probe.finish(sums_out)
+        sums_out[...] = probe.finish()[...]
         for h in range(2):
             strip.end(h)
         for h in range(2):
@@ -648,9 +646,11 @@
         gather_kernel,
         out_shape=[jax.ShapeDtypeStruct((GROUPS, OTILES, 8, WIN), f32), jax.ShapeDtypeStruct(halves, f32)]
         + [jax.ShapeDtypeStruct(array.shape, jnp.int32) for array in offsets],
-        in_specs=[VMEM] + [ANY] * 4,
+        in_specs=[ANY] * 5,
         out_specs=[ANY] * 5,
-        scratch_shapes=[pltpu.VMEM((2, OTILES, 8, WIN), f32), dma(copies), dma(copies), pltpu.SemaphoreType.DMA],
+        scratch_shapes=[
+            pltpu.VMEM(object_field.shape, f32), pltpu.VMEM((2, OTILES, 8, WIN), f32), dma(copies), dma(copies), pltpu.SemaphoreType.DMA,
+        ],
         compiler_params=params(0),
         name="gather_object",
     )(object_field, amplitudes, *offsets)
@@ -659,19 +659,17 @@
 def exchange(sums, probe_sums, strip, probe, object_shape):
     tiles = lax.axis_size("tile")
     is_last = probe is not None
-    by_device = (RING, RING, 2, 2, 8, WIN)
     if is_last:
         out_shape = (jax.ShapeDtypeStruct(object_shape, f32), jax.ShapeDtypeStruct(probe.shape, f32))
         out_specs = (VMEM, VMEM)
     else:
-        out_shape = (jax.ShapeDtypeStruct(strip.shape, f32), jax.ShapeDtypeStruct(by_device, f32))
+        out_shape = (jax.ShapeDtypeStruct(strip.shape, f32), jax.ShapeDtypeStruct((PTILES, 8, WIN), f32))
         out_specs = (ANY, VMEM)
-    group, pair = (STILES, 8, WIN), (2, 8, WIN)
+    group, part = (STILES, 8, WIN), (PTILES // 2 // tiles, 8, WIN)
     buffers = [
         (2, OTILES, 8, WIN), (2, RING, RING) + group, (2, RING, RING) + group, (2, 3, RING) + group, (2, 3) + group,
         (2, 2, RING, STILES // 2, 8, WIN), (2, OTILES, 8, WIN),
-        (RING, RING) + pair, (RING, RING) + pair, (RING, RING) + pair, (3, RING) + pair, (RING,) + pair, (3,) + pair,
-        (tiles,) + pair, (RING, RING) + pair, (RING, RING) + pair, by_device,
+        (PTILES // 2, 8, WIN), (PTILES // 2, 8, WIN), (tiles - 1,) + part, (RING,) + part, (RING,) + part, (PTILES, 8, WIN),
     ]
     return pl.pallas_call(
         functools.partial(exchange_kernel, tiles, is_last),
@@ -680,10 +678,10 @@
         out_specs=out_specs,
         scratch_shapes=[pltpu.VMEM(shape, f32) for shape in buffers]
         + [dma(RING * RING), dma(4)]
-        + [dma(REDUCE_COPIES)] * 2 + [dma(GATHER_COPIES)] * 2 + [dma(14 + tiles - 1)] * 2,
+        + [dma(REDUCE_COPIES)] * 2 + [dma(GATHER_COPIES)] * 2 + [dma(8 + 2 * (tiles - 1))] * 2,
         compiler_params=params(2 if is_last else 1),
         name="exchange_last" if is_last else "exchange_middle",
-    )(sums, probe_sums.reshape(by_device), strip, *([probe] if is_last else []))
+    )(sums, probe_sums, strip, *([probe] if is_last else []))
 
 
 def per_device(object_field, illumination, row_offsets, col_offsets, counts, amplitudes):
@@ -691,15 +689,18 @@
     offsets = [row_offsets, col_offsets, counts.T]
     iterations, cap = row_offsets.shape
     amplitudes = amplitudes.reshape(iterations, cap // 2, 2, WIN, WIN)
-    strip, amplitudes_in, *offsets_in = gather_object(object_field, amplitudes, offsets)
-    probe, old_sums = illumination, None
+    first, probe, tables, amplitudes, *offsets = (
+        pltpu.with_memory_space_constraint(array, pltpu.HBM)
+        for array in [object_field, illumination, tables, amplitudes, *offsets]
+    )
+    strip, amplitudes_in, *offsets_in = gather_object(first, amplitudes, offsets)
+    old_sums = None
     for iteration in range(iterations):
         sums, probe_sums, probe = sweep(
             iteration, strip, probe, old_sums, offsets + offsets_in, amplitudes, amplitudes_in, tables
         )
         if iteration + 1 < iterations:
             strip, old_sums = exchange(sums, probe_sums, strip, None, None)
-            old_sums = old_sums.reshape(GROUPS, 8, WIN)
     return exchange(sums, probe_sums, strip, probe, object_field.shape)
 
 

time: 127 us -> 114 us (0.90)
  Pallas kernels: 123 us -> 112 us
  local copies, waits for them, and re-layouts: 3.04 us -> 1.29 us
    pallas_call x2, Pallas kernels: 21.2 us -> 13.4 us  [sweep(): pl.pallas_call(functools.partial(sweep_kernel, iteration, updates), out_s...]
    unnamed x2, local copies, waits for them, and re-layouts: 3.04 us -> 1.29 us
    pallas_call x2, Pallas kernels: 80.8 us -> 79.3 us  [exchange(): pl.pallas_call(functools.partial(exchange_kernel, tiles, is_last), out_sh...]
where the time goes in v3:
time: 114 us
  Pallas kernels  112 us (98%)
  local copies, waits for them, and re-layouts  1.29 us (1%)
    pallas_call x2, Pallas kernels, exchange(): pl.pallas_call(functools.partial(exchange_kernel, tiles, is_last), out_sh...  79.3 us
    pallas_call x1, Pallas kernels, gather_object(): pl.pallas_call(gather_kernel, out_shape=[jax.ShapeDtypeStruct((GROUPS, OT...  19.6 us
    pallas_call x2, Pallas kernels, sweep(): pl.pallas_call(functools.partial(sweep_kernel, iteration, updates), out_s...  13.4 us

profile of v3, /device:TPU:1, one launch (start us, length us, event | category | flops | bytes accessed | tf_op | source)
XLA Modules:
  0.0 114.3 jit_solution(1103442411582589793)
XLA Ops:
  0.6 19.6 %gather_object.1 = (f32[64,8,8,128]{3,2,1,0:T(8,128)S(1)}, f32[2,16,128,128]{3,2,1,0:T(8,128)S(1)}, s32[2,32]{1,0:T(2,128)S(1)}, s32[2,32]{1,0:T(2,128)S(1)}, s32[1,2]{1,0:T(1,128)S(1)}) custom-call(f32[2,16,512]{2,1,0:T(8,128)} %object_hbm.1, f32[2,16,2,128,128]{4,3,2,1,0:T(8,128)} %bitcast.2, s32[2,32]{1,0:T(2,128)} %rows_hbm.5, s32[2,32]{1,0:T(2,128)} %cols_hbm.5, ...), custom_call_target="tpu_custom_call" | custom-call | tf_op jit(solution)/shard_map/gather_object/pallas_call | solution.py:645
  20.2 5.6 %sweep.2 = (f32[64,12,8,128]{3,2,1,0:T(8,128)S(1)}, f32[48,8,128]{2,1,0:T(8,128)S(1)}, f32[2,128,128]{2,1,0:T(8,128)S(1)}) custom-call(s32[2,32]{1,0:T(2,128)} %rows_hbm.5, s32[2,32]{1,0:T(2,128)} %cols_hbm.5, s32[1,2]{1,0:T(1,128)} %bitcast.6, s32[2,32]{1,0:T(2,128)S(1)} %get-tuple-element.15.rows_in, s32[2,32]{1,0:T(2,128)S(1)} %get-tuple-element.16.cols_in, ...), custom_call_target="tpu_custom_call" | custom-call | tf_op jit(solution)/shard_map/sweep/pallas_call | solution.py:209
  25.9 46.3 %exchange_middle.1 = (f32[64,8,8,128]{3,2,1,0:T(8,128)S(1)}, f32[48,8,128]{2,1,0:T(8,128)S(1)}) custom-call(f32[64,12,8,128]{3,2,1,0:T(8,128)S(1)} %get-tuple-element.21.sums_hbm, f32[48,8,128]{2,1,0:T(8,128)S(1)} %get-tuple-element.22.probe_src, f32[64,8,8,128]{3,2,1,0:T(8,128)S(1)} %get-tuple-element.18.strip_hbm), custom_call_target="tpu_custom_call" | custom-call | tf_op jit(solution)/shard_map/exchange_middle/pallas_call | solution.py:674
  72.2 7.8 %sweep.3 = (f32[64,12,8,128]{3,2,1,0:T(8,128)S(1)}, f32[48,8,128]{2,1,0:T(8,128)S(1)}, f32[2,128,128]{2,1,0:T(8,128)S(1)}) custom-call(s32[2,32]{1,0:T(2,128)} %rows_hbm.5, s32[2,32]{1,0:T(2,128)} %cols_hbm.5, s32[1,2]{1,0:T(1,128)} %bitcast.7, s32[2,32]{1,0:T(2,128)S(1)} %get-tuple-element.15.rows_in, s32[2,32]{1,0:T(2,128)S(1)} %get-tuple-element.16.cols_in, ...), custom_call_target="tpu_custom_call" | custom-call | tf_op jit(solution)/shard_map/sweep/pallas_call | solution.py:209
  80.0 33.0 %exchange_last.1 = (f32[2,16,512]{2,1,0:T(8,128)S(1)}, f32[2,128,128]{2,1,0:T(8,128)S(1)}) custom-call(f32[64,12,8,128]{3,2,1,0:T(8,128)S(1)} %get-tuple-element.25.sums_hbm, f32[48,8,128]{2,1,0:T(8,128)S(1)} %get-tuple-element.26.probe_src, f32[64,8,8,128]{3,2,1,0:T(8,128)S(1)} %get-tuple-element.24.strip_hbm, f32[2,128,128]{2,1,0:T(8,128)S(1)} %get-tuple-element.27.refs_0_), custom_call_target="tpu_custom_call" | custom-call | tf_op jit(solution)/shard_map/exchange_last/pallas_call | solution.py:674
  113.0 0.6 copy.11
  113.6 0.7 copy.12

commit v4 on v3

--- a/solution.py
+++ b/solution.py
@@ -65,10 +65,9 @@
 
 def sweep_kernel(
     iteration, updates,
-    rows_hbm, cols_hbm, counts_hbm, rows_in, cols_in, counts_in, probe_hbm, old_hbm, tables_hbm, strip_hbm,
-    amp_hbm, amp_in, out_hbm, sums_out, probe_out,
-    rows, cols, counts, rows2, cols2, counts2, tables, split_tables, probe, old_sums, strip, sums, amp, probe_sums,
-    small_sem, strip_sem, amp_sem, out_sem,
+    rows_hbm, cols_hbm, counts_hbm, rows_in, cols_in, counts_in, probe_hbm, old_hbm, tables_hbm, strip,
+    amp_hbm, amp_in, sums, probe_sums, probe_out,
+    rows, cols, counts, rows2, cols2, counts2, tables, split_tables, probe, old_sums, amp, small_sem, amp_sem,
 ):
     half = amp.shape[0] // 2
     core = lax.axis_index("pos") % 2
@@ -79,7 +78,8 @@
     if updates:
         small.append((old_hbm, old_sums))
     copies = [pltpu.make_async_copy(src, dst, small_sem.at[k]) for k, (src, dst) in enumerate(small)]
-    copies += [pltpu.make_async_copy(strip_hbm.at[:, k], strip.at[k], strip_sem.at[k]) for k in range(OTILES)]
+    for source, src in enumerate((amp_hbm.at[iteration, :, core], amp_in.at[iteration])):
+        copies.append(pltpu.make_async_copy(src, amp.at[pl.ds(source * half, half)], amp_sem.at[source]))
     for copy in copies:
         copy.start()
     sums_rows = sums.reshape(STILES, ROWS, WIN)
@@ -89,21 +89,10 @@
         sums_rows[k] = jnp.zeros((ROWS, WIN), f32)
     for k in range(3):
         probe_rows[k] = jnp.zeros((WIN, WIN), f32)
-    for copy in copies[:2]:
+    for copy in copies:
         copy.wait()
     mine = (counts[0, iteration] + 1 - core) // 2
     count = mine + (counts2[0, iteration] + 1 - core) // 2
-    amp_copies = []
-    for source, live in ((0, mine), (1, count - mine)):
-        for k in range(half // GRAIN):
-            part, at = pl.ds(k * GRAIN, GRAIN), pl.ds(source * half + k * GRAIN, GRAIN)
-            src = amp_in.at[iteration, part] if source else amp_hbm.at[iteration, part, core]
-            copy = pltpu.make_async_copy(src, amp.at[at], amp_sem.at[source, k])
-            amp_copies.append((live > k * GRAIN, copy))
-    for needed, copy in amp_copies:
-        pl.when(needed)(copy.start)
-    for copy in copies[2:]:
-        copy.wait()
     if updates:
         stepped = probe_step(probe, old_sums.reshape(3, WIN, WIN))
         for k in range(2):
@@ -111,8 +100,6 @@
     probe_out[...] = probe[...]
     for k in range(2):
         split_tables[k, : 2 * WIN], split_tables[k, 2 * WIN :] = split(tables[k])
-    for needed, copy in amp_copies:
-        pl.when(needed)(copy.wait)
     lane = lax.broadcasted_iota(jnp.int32, (WIN, WIN), 1)
 
     def work(begin, size):
@@ -185,15 +172,8 @@
     whole = (count + BLOCK // 2 - 1) // BLOCK
     lax.fori_loop(0, whole, body, 0)
     pl.when(count > whole * BLOCK)(lambda: work(whole * BLOCK, BLOCK // 2))
-    outs = [pltpu.make_async_copy(sums.at[k], out_hbm.at[:, k], out_sem.at[k]) for k in range(STILES)]
-    outs.append(pltpu.make_async_copy(probe_sums, sums_out, out_sem.at[STILES]))
-    for copy in outs:
-        copy.start()
-    for copy in outs:
-        copy.wait()
-
-
-GRAIN = 4
+
+
 VMEM_BYTES = 20 * 1024 * 1024
 ANY = pl.BlockSpec(memory_space=pl.ANY)
 VMEM = pl.BlockSpec(memory_space=pltpu.VMEM)
@@ -209,26 +189,21 @@
     return pl.pallas_call(
         functools.partial(sweep_kernel, iteration, updates),
         out_shape=(
-            jax.ShapeDtypeStruct((GROUPS, STILES, 8, WIN), f32),
+            jax.ShapeDtypeStruct((STILES, GROUPS, 8, WIN), f32),
             jax.ShapeDtypeStruct((PTILES, 8, WIN), f32),
             jax.ShapeDtypeStruct(probe.shape, f32),
         ),
-        in_specs=[ANY] * 12,
-        out_specs=(ANY, ANY, VMEM),
+        in_specs=[ANY] * 9 + [VMEM] + [ANY] * 2,
+        out_specs=(VMEM, VMEM, VMEM),
         scratch_shapes=[pltpu.SMEM(array.shape, jnp.int32) for array in offsets]
         + [
             pltpu.VMEM(tables.shape, f32),
             pltpu.VMEM((2, 4 * WIN, 2 * WIN), jnp.bfloat16),
             pltpu.VMEM(probe.shape, f32),
             pltpu.VMEM((PTILES, 8, WIN), f32),
-            pltpu.VMEM((OTILES, GROUPS, 8, WIN), f32),
-            pltpu.VMEM((STILES, GROUPS, 8, WIN), f32),
             pltpu.VMEM((cap, WIN, WIN), f32),
-            pltpu.VMEM((PTILES, 8, WIN), f32),
             dma(10),
-            dma(OTILES),
-            dma(2, cap // 2 // GRAIN),
-            dma(STILES + 1),
+            dma(2),
         ],
         compiler_params=pltpu.CompilerParams(vmem_limit_bytes=VMEM_BYTES),
         name="sweep",
@@ -311,22 +286,21 @@
     def load(self):
         for far in ALL:
             for near in ALL:
-                copy = pltpu.make_async_copy(
-                    self.src.at[pl.ds(2 * self.place.at(near, far), 2)], self.own.at[:, near, far],
-                    self.load_sem.at[4 * near + far])
-                copy.start()
-                self.loads[near, far] = copy
+                for h in range(2):
+                    src = self.src.at[:, 2 * self.place.at(near, far) + h]
+                    sem = self.load_sem.at[2 * (4 * near + far) + h]
+                    copy = pltpu.make_async_copy(src, self.own.at[h, near, far], sem)
+                    copy.start()
+                    self.loads[h, near, far] = copy
 
     def core_send(self, h):
         for far in ALL:
             for near in ALL:
-                self.sender.send(("core", h, near, far), self.src.at[2 * self.place.other_at(near, far) + h],
+                self.sender.send(("core", h, near, far), self.src.at[:, 2 * self.place.other_at(near, far) + h],
                                  self.core_in.at[h, near, far], self.place.other())
 
     def pair(self, h, near, far):
-        copy = self.loads.pop((near, far), None)
-        if copy is not None:
-            copy.wait()
+        self.loads[h, near, far].wait()
         self.sender.arrive(("core", h, near, far), self.core_in.at[h, near, far], self.place.other())
         self.own[h, near, far] += self.core_in[h, near, far]
 
@@ -388,10 +362,10 @@
         self.place, self.sender, self.buf, self.name = place, sender, buf, name
 
     def at(self, h, near, far):
-        return self.buf.at[2 * self.place.at(near, far) + h]
+        return self.buf.at[:, 2 * self.place.at(near, far) + h]
 
     def spread(self, h, near):
-        for far in (1, 3) if near in self.relays else AWAY:
+        for far in AWAY:
             self.sender.send((self.name, "far", h, near, far), self.at(h, near, 0), self.at(h, near, 0), self.place.far_peer(far))
 
     def to_core(self, h, near, far):
@@ -402,24 +376,6 @@
             self.sender.send((self.name, "near", h, near), self.at(h, 0, 0), self.at(h, 0, 0), self.place.near_peer(near))
         self.spread(h, 0)
         self.to_core(h, 0, 0)
-
-    relays = ()
-
-    def half(self, h, near, far, k):
-        return self.buf.at[2 * self.place.at(near, far) + h, pl.ds(4 * k, 4)]
-
-    def relay(self, h, near):
-        for k, far in enumerate((1, 3)):
-            back = RING - far
-            self.sender.arrive((self.name, "far", h, near, far), self.at(h, near, back), self.place.far_peer(back))
-            at = self.half(h, near, back, k)
-            self.sender.send((self.name, "relay", h, near, far), at, at, self.place.far_peer(far))
-            self.to_core(h, near, back)
-
-    def relayed(self, h, near):
-        for k, far in enumerate((1, 3)):
-            self.sender.arrive((self.name, "relay", h, near, far), self.half(h, near, 2, k), self.place.far_peer(RING - far))
-        self.to_core(h, near, 2)
 
     def middle(self, h):
         for near in (1, 3, 2):
@@ -429,21 +385,15 @@
             self.to_core(h, near, 0)
 
     def end(self, h, nears=(0, 1, 3, 2)):
-        for near in self.relays:
-            self.relay(h, near)
         for near in nears:
-            if near in self.relays:
-                continue
             for far in (1, 3, 2):
                 self.sender.arrive((self.name, "far", h, near, RING - far), self.at(h, near, far), self.place.far_peer(far))
                 self.to_core(h, near, far)
 
     def done(self, h):
-        for near in self.relays:
-            self.relayed(h, near)
         for near in range(RING):
             for far in range(RING):
-                at = self.buf.at[2 * self.place.other_at(near, far) + h]
+                at = self.buf.at[:, 2 * self.place.other_at(near, far) + h]
                 self.sender.arrive((self.name, "core", h, near, far), at, self.place.other())
 
 
@@ -530,8 +480,8 @@
     for g in range(2):
         for p in range(2):
             for b in range(COLS):
-                mine[g, COLS * p + b] = object_ref[p, 8 * g : 8 * g + 8, WIN * b : WIN * b + WIN]
-    copy = pltpu.make_async_copy(mine, out_hbm.at[pl.ds(2 * place.at(0, 0), 2)], copy_sem)
+                mine[COLS * p + b, g] = object_ref[p, 8 * g : 8 * g + 8, WIN * b : WIN * b + WIN]
+    copy = pltpu.make_async_copy(mine, out_hbm.at[:, pl.ds(2 * place.at(0, 0), 2)], copy_sem)
     copy.start()
     greet(place, 1)
     copy.wait()
@@ -569,7 +519,7 @@
      load_sem, copy_sem, send_sem, recv_sem, send_sem2, recv_sem2, send_sem3, recv_sem3) = refs
     place = Place()
     here = pl.ds(2 * place.at(0, 0), 2)
-    load = pltpu.make_async_copy(strip_hbm.at[here], old, copy_sem.at[0])
+    load = pltpu.make_async_copy(strip_hbm.at[:, here], old, copy_sem.at[0])
     load.start()
     first, second, third = Sender(send_sem, recv_sem), Sender(send_sem2, recv_sem2), Sender(send_sem3, recv_sem3)
     sums = Reduce(place, first, sums_hbm, own, core_in, far_in, near_in, load_sem)
@@ -601,13 +551,13 @@
         for b in range(COLS):
             scale = 1.0 / (total[2 * COLS + b] + 1.0)
             for p in range(2):
-                tile = (old[h, COLS * p + b] + total[COLS * p + b]) * scale
+                tile = (old[COLS * p + b, h] + total[COLS * p + b]) * scale
                 if last:
                     object_out[p, 8 * h : 8 * h + 8, WIN * b : WIN * b + WIN] = tile
                 else:
-                    mine[h, COLS * p + b] = tile
+                    mine[COLS * p + b, h] = tile
         if not last:
-            copy = pltpu.make_async_copy(mine.at[h], strip.at(h, 0, 0), copy_sem.at[1 + h])
+            copy = pltpu.make_async_copy(mine.at[:, h], strip.at(h, 0, 0), copy_sem.at[1 + h])
             copy.start()
             copy.wait()
             strip.start(h)
@@ -644,12 +594,12 @@
     halves = amplitudes.shape[:2] + amplitudes.shape[3:]
     return pl.pallas_call(
         gather_kernel,
-        out_shape=[jax.ShapeDtypeStruct((GROUPS, OTILES, 8, WIN), f32), jax.ShapeDtypeStruct(halves, f32)]
+        out_shape=[jax.ShapeDtypeStruct((OTILES, GROUPS, 8, WIN), f32), jax.ShapeDtypeStruct(halves, f32)]
         + [jax.ShapeDtypeStruct(array.shape, jnp.int32) for array in offsets],
         in_specs=[ANY] * 5,
         out_specs=[ANY] * 5,
         scratch_shapes=[
-            pltpu.VMEM(object_field.shape, f32), pltpu.VMEM((2, OTILES, 8, WIN), f32), dma(copies), dma(copies), pltpu.SemaphoreType.DMA,
+            pltpu.VMEM(object_field.shape, f32), pltpu.VMEM((OTILES, 2, 8, WIN), f32), dma(copies), dma(copies), pltpu.SemaphoreType.DMA,
         ],
         compiler_params=params(0),
         name="gather_object",
@@ -667,8 +617,8 @@
         out_specs = (ANY, VMEM)
     group, part = (STILES, 8, WIN), (PTILES // 2 // tiles, 8, WIN)
     buffers = [
-        (2, OTILES, 8, WIN), (2, RING, RING) + group, (2, RING, RING) + group, (2, 3, RING) + group, (2, 3) + group,
-        (2, 2, RING, STILES // 2, 8, WIN), (2, OTILES, 8, WIN),
+        (OTILES, 2, 8, WIN), (2, RING, RING) + group, (2, RING, RING) + group, (2, 3, RING) + group, (2, 3) + group,
+        (2, 2, RING, STILES // 2, 8, WIN), (OTILES, 2, 8, WIN),
         (PTILES // 2, 8, WIN), (PTILES // 2, 8, WIN), (tiles - 1,) + part, (RING,) + part, (RING,) + part, (PTILES, 8, WIN),
     ]
     return pl.pallas_call(
@@ -677,7 +627,7 @@
         in_specs=[ANY, ANY, ANY] + ([VMEM] if is_last else []),
         out_specs=out_specs,
         scratch_shapes=[pltpu.VMEM(shape, f32) for shape in buffers]
-        + [dma(RING * RING), dma(4)]
+        + [dma(2 * RING * RING), dma(4)]
         + [dma(REDUCE_COPIES)] * 2 + [dma(GATHER_COPIES)] * 2 + [dma(8 + 2 * (tiles - 1))] * 2,
         compiler_params=params(2 if is_last else 1),
         name="exchange_last" if is_last else "exchange_middle",

time: 114 us -> 110 us (0.965)
  Pallas kernels: 112 us -> 108 us
    pallas_call x2, Pallas kernels: 79.3 us -> 77 us  [exchange(): pl.pallas_call(functools.partial(exchange_kernel, tiles, is_last), out_sh...]
    pallas_call x2, Pallas kernels: 13.4 us -> 11.2 us  [sweep(): pl.pallas_call(functools.partial(sweep_kernel, iteration, updates), out_s...]
where the time goes in v4:
time: 110 us
  Pallas kernels  108 us (98%)
  local copies, waits for them, and re-layouts  1.29 us (1%)
    pallas_call x2, Pallas kernels, exchange(): pl.pallas_call(functools.partial(exchange_kernel, tiles, is_last), out_sh...  77 us
    pallas_call x1, Pallas kernels, gather_object(): pl.pallas_call(gather_kernel, out_shape=[jax.ShapeDtypeStruct((OTILES, GR...  19.5 us
    pallas_call x2, Pallas kernels, sweep(): pl.pallas_call(functools.partial(sweep_kernel, iteration, updates), out_s...  11.2 us

profile of v4, /device:TPU:1, one launch (start us, length us, event | category | flops | bytes accessed | tf_op | source)
XLA Modules:
  0.0 109.7 jit_solution(6505145342547216063)
XLA Ops:
  0.6 19.5 %gather_object.1 = (f32[8,64,8,128]{3,2,1,0:T(8,128)S(1)}, f32[2,16,128,128]{3,2,1,0:T(8,128)S(1)}, s32[2,32]{1,0:T(2,128)S(1)}, s32[2,32]{1,0:T(2,128)S(1)}, s32[1,2]{1,0:T(1,128)S(1)}) custom-call(f32[2,16,512]{2,1,0:T(8,128)} %object_hbm.1, f32[2,16,2,128,128]{4,3,2,1,0:T(8,128)} %bitcast.2, s32[2,32]{1,0:T(2,128)} %rows_hbm.5, s32[2,32]{1,0:T(2,128)} %cols_hbm.5, ...), custom_call_target="tpu_custom_call" | custom-call | tf_op jit(solution)/shard_map/gather_object/pallas_call | solution.py:595
  20.2 6.3 %sweep.2 = (f32[12,64,8,128]{3,2,1,0:T(8,128)S(1)}, f32[48,8,128]{2,1,0:T(8,128)S(1)}, f32[2,128,128]{2,1,0:T(8,128)S(1)}) custom-call(s32[2,32]{1,0:T(2,128)} %rows_hbm.5, s32[2,32]{1,0:T(2,128)} %cols_hbm.5, s32[1,2]{1,0:T(1,128)} %bitcast.6, s32[2,32]{1,0:T(2,128)S(1)} %get-tuple-element.15.rows_in, s32[2,32]{1,0:T(2,128)S(1)} %get-tuple-element.16.cols_in, ...), custom_call_target="tpu_custom_call" | custom-call | tf_op jit(solution)/shard_map/sweep/pallas_call | solution.py:189
  26.5 43.6 %exchange_middle.1 = (f32[8,64,8,128]{3,2,1,0:T(8,128)S(1)}, f32[48,8,128]{2,1,0:T(8,128)S(1)}) custom-call(f32[12,64,8,128]{3,2,1,0:T(8,128)S(1)} %get-tuple-element.21.sums_hbm, f32[48,8,128]{2,1,0:T(8,128)S(1)} %get-tuple-element.22.probe_src, f32[8,64,8,128]{3,2,1,0:T(8,128)S(1)} %get-tuple-element.18.strip.strip_hbm), custom_call_target="tpu_custom_call" | custom-call | tf_op jit(solution)/shard_map/exchange_middle/pallas_call | solution.py:624
  70.1 4.9 %sweep.3 = (f32[12,64,8,128]{3,2,1,0:T(8,128)S(1)}, f32[48,8,128]{2,1,0:T(8,128)S(1)}, f32[2,128,128]{2,1,0:T(8,128)S(1)}) custom-call(s32[2,32]{1,0:T(2,128)} %rows_hbm.5, s32[2,32]{1,0:T(2,128)} %cols_hbm.5, s32[1,2]{1,0:T(1,128)} %bitcast.7, s32[2,32]{1,0:T(2,128)S(1)} %get-tuple-element.15.rows_in, s32[2,32]{1,0:T(2,128)S(1)} %get-tuple-element.16.cols_in, ...), custom_call_target="tpu_custom_call" | custom-call | tf_op jit(solution)/shard_map/sweep/pallas_call | solution.py:189
  75.0 33.4 %exchange_last.1 = (f32[2,16,512]{2,1,0:T(8,128)S(1)}, f32[2,128,128]{2,1,0:T(8,128)S(1)}) custom-call(f32[12,64,8,128]{3,2,1,0:T(8,128)S(1)} %get-tuple-element.25.sums_hbm, f32[48,8,128]{2,1,0:T(8,128)S(1)} %get-tuple-element.26.probe_src, f32[8,64,8,128]{3,2,1,0:T(8,128)S(1)} %get-tuple-element.24.strip.strip_hbm, ...), custom_call_target="tpu_custom_call" | custom-call | tf_op jit(solution)/shard_map/exchange_last/pallas_call | solution.py:624
  108.4 0.6 copy.11
  109.1 0.7 copy.12

commit v5 on v4

--- a/solution.py
+++ b/solution.py
@@ -46,8 +46,7 @@
 
 def along_columns(pairs, table):
     high, low = blocks(pairs)
-    both = dot(jnp.concatenate([high, low], 0), table[: 2 * WIN])
-    return both[: 2 * WIN] + both[2 * WIN :] + dot(high, table[2 * WIN :])
+    return dot(jnp.concatenate([high, high], 1), table) + dot(low, table[: 2 * WIN])
 
 
 def along_rows(y, table):
@@ -67,7 +66,7 @@
     iteration, updates,
     rows_hbm, cols_hbm, counts_hbm, rows_in, cols_in, counts_in, probe_hbm, old_hbm, tables_hbm, strip,
     amp_hbm, amp_in, sums, probe_sums, probe_out,
-    rows, cols, counts, rows2, cols2, counts2, tables, split_tables, probe, old_sums, amp, small_sem, amp_sem,
+    rows, cols, counts, rows2, cols2, counts2, tables, split_tables, probe, old_sums, power, amp, small_sem, amp_sem,
 ):
     half = amp.shape[0] // 2
     core = lax.axis_index("pos") % 2
@@ -98,11 +97,14 @@
         for k in range(2):
             probe[k] = stepped[k]
     probe_out[...] = probe[...]
+    power[...] = probe[0] * probe[0] + probe[1] * probe[1]
     for k in range(2):
         split_tables[k, : 2 * WIN], split_tables[k, 2 * WIN :] = split(tables[k])
     lane = lax.broadcasted_iota(jnp.int32, (WIN, WIN), 1)
 
     def work(begin, size):
+        windows = {}
+
         def find(number):
             theirs = number >= mine
             place = jnp.minimum(jnp.where(theirs, number - mine, number), half - 1)
@@ -123,7 +125,8 @@
             return here, q, [pltpu.roll(probe[p], turn, 1) for p in range(2)]
 
         def exit_wave(found):
-            _, (qr, qi), (pr, pi) = window(found)
+            windows[id(found)] = window(found)
+            _, (qr, qi), (pr, pi) = windows[id(found)]
             return pr * qr - pi * qi, pr * qi + pi * qr
 
         def scaled(found, z):
@@ -135,10 +138,10 @@
 
         def add(found, g):
             number, _, row, first, second, turn = found
-            here, (qr, qi), (pr, pi) = window(found)
+            here, (qr, qi), (pr, pi) = windows[id(found)]
             gr, gi = g
             live = (number < count).astype(f32)
-            for p, term in enumerate((pr * gr + pi * gi, pr * gi - pi * gr, (pr * pr + pi * pi) * live)):
+            for p, term in enumerate((pr * gr + pi * gi, pr * gi - pi * gr, (pltpu.roll(power[...], turn, 1)) * live)):
                 sums_rows[COLS * p + first, row, :] += jnp.where(here, term, 0.0)
                 sums_rows[COLS * p + second, row, :] += jnp.where(here, 0.0, term)
             back = jnp.where(turn == 0, 0, WIN - turn)
@@ -201,6 +204,7 @@
             pltpu.VMEM((2, 4 * WIN, 2 * WIN), jnp.bfloat16),
             pltpu.VMEM(probe.shape, f32),
             pltpu.VMEM((PTILES, 8, WIN), f32),
+            pltpu.VMEM((WIN, WIN), f32),
             pltpu.VMEM((cap, WIN, WIN), f32),
             dma(10),
             dma(2),
@@ -240,17 +244,17 @@
     def other(self):
         return {"pos": self.other_at(0, 0)}
 
-    def tile_peer(self, k, tiles):
-        return {"tile": (self.tile + k) % tiles}
+    def tile_peer(self, k, tiles, other):
+        return {"tile": (self.tile + k) % tiles, "pos": self.other_at(0, 0) if other else self.at(0, 0)}
 
 
 def greet(place, tiles):
     barrier = pltpu.get_barrier_semaphore()
     peers = [place.other()] + [place.near_peer(k) for k in AWAY] + [place.far_peer(k) for k in AWAY]
-    peers += [place.tile_peer(k, tiles) for k in range(1, tiles)]
+    peers += [place.tile_peer(k, tiles, other) for other in range(2) for k in range(1, tiles)]
     for peer in peers:
         pl.semaphore_signal(barrier, inc=1, device_id=peer, device_id_type=MESH)
-    pl.semaphore_wait(barrier, len(peers))
+    return lambda: pl.semaphore_wait(barrier, len(peers))
 
 
 class Sender:
@@ -278,20 +282,9 @@
 
 
 class Reduce:
-    def __init__(self, place, sender, src, own, core_in, far_in, near_in, load_sem, relay=False):
+    def __init__(self, place, sender, src, own, core_in, far_in, near_in, relay_in):
         self.place, self.sender, self.src, self.own = place, sender, src, own
-        self.core_in, self.far_in, self.near_in, self.load_sem = core_in, far_in, near_in, load_sem
-        self.loads = {}
-
-    def load(self):
-        for far in ALL:
-            for near in ALL:
-                for h in range(2):
-                    src = self.src.at[:, 2 * self.place.at(near, far) + h]
-                    sem = self.load_sem.at[2 * (4 * near + far) + h]
-                    copy = pltpu.make_async_copy(src, self.own.at[h, near, far], sem)
-                    copy.start()
-                    self.loads[h, near, far] = copy
+        self.core_in, self.far_in, self.near_in, self.relay_in = core_in, far_in, near_in, relay_in
 
     def core_send(self, h):
         for far in ALL:
@@ -300,18 +293,9 @@
                                  self.core_in.at[h, near, far], self.place.other())
 
     def pair(self, h, near, far):
-        self.loads[h, near, far].wait()
         self.sender.arrive(("core", h, near, far), self.core_in.at[h, near, far], self.place.other())
-        self.own[h, near, far] += self.core_in[h, near, far]
-
-    def far_send(self, h, fars=AWAY):
-        for far in fars:
-            for near in ALL:
-                self.pair(h, near, far)
-                self.sender.send(("far", h, near, far), self.own.at[h, near, far], self.far_in.at[h, far - 1, near],
-                                 self.place.far_peer(far))
-
-    relay_in = None
+        mine = self.src[:, 2 * self.place.at(near, far) + h]
+        self.own[h, near, far] = mine + self.core_in[h, near, far]
 
     def far_first(self, h):
         for near in ALL:
@@ -335,7 +319,7 @@
     def line(self, h, near):
         self.pair(h, near, 0)
         total = self.own[h, near, 0]
-        for far in (1, 3) if self.relay_in is not None else (1, 3, 2):
+        for far in (1, 3):
             at = self.far_in.at[h, far - 1, near]
             self.sender.arrive(("far", h, near, far), at, self.place.far_peer(RING - far))
             total = total + at[...]
@@ -398,30 +382,23 @@
 
 
 class ProbeSum:
-    def __init__(self, place, sender, src, tiles, own, core_in, tile_in, x_in, y_in, total, load_sem):
-        self.place, self.sender, self.src, self.tiles, self.own, self.core_in = place, sender, src, tiles, own, core_in
-        self.tile_in, self.x_in, self.y_in, self.total, self.load_sem = tile_in, x_in, y_in, total, load_sem
-        self.half = PTILES // 2
-        self.part = self.half // tiles
-
-    def tiles_of(self, core):
-        return pl.ds(core * self.half, self.half)
-
-    def load(self):
-        self.copy = pltpu.make_async_copy(self.src.at[self.tiles_of(self.place.core)], self.own, self.load_sem)
-        self.copy.start()
-
-    def core(self):
-        self.sender.send("core", self.src.at[self.tiles_of(1 - self.place.core)], self.core_in, self.place.other())
+    def __init__(self, place, sender, src, tiles, tile_in, x_in, y_in, total):
+        self.place, self.sender, self.src, self.tiles = place, sender, src, tiles
+        self.tile_in, self.x_in, self.y_in, self.total = tile_in, x_in, y_in, total
+        self.part = PTILES // 2 // tiles
+        self.others = [(other, k) for k in range(tiles) for other in range(2) if other or k]
+
+    def share(self, other, k):
+        core = 1 - self.place.core if other else self.place.core
+        return pl.ds(((self.place.tile + k) % self.tiles + core * self.tiles) * self.part, self.part)
+
+    def peer(self, other, k):
+        return self.place.tile_peer(k, self.tiles, other)
 
     def across(self):
-        place = self.place
-        self.copy.wait()
-        self.sender.arrive("core", self.core_in, place.other())
-        self.own[...] += self.core_in[...]
-        for k in range(1, self.tiles):
-            src = self.own.at[pl.ds((place.tile + k) % self.tiles * self.part, self.part)]
-            self.sender.send(("tile", k), src, self.tile_in.at[k - 1], place.tile_peer(k, self.tiles))
+        for other, k in self.others:
+            src, dst = self.src.at[self.share(other, k)], self.tile_in.at[2 * k + other]
+            self.sender.send(("tile", other, k), src, dst, self.peer(other, k))
 
     def spread(self, name, buf, at, peer):
         for k in AWAY:
@@ -434,10 +411,11 @@
 
     def along_x(self):
         place = self.place
-        total = self.own[pl.ds(place.tile * self.part, self.part)]
-        for k in range(1, self.tiles):
-            self.sender.arrive(("tile", k), self.tile_in.at[k - 1], place.tile_peer(self.tiles - k, self.tiles))
-            total = total + self.tile_in[k - 1]
+        total = self.src[self.share(0, 0)]
+        for other, k in self.others:
+            at = self.tile_in.at[2 * k + other]
+            self.sender.arrive(("tile", other, k), at, self.peer(other, self.tiles - k))
+            total = total + at[...]
         self.x_in[place.x] = total
         self.spread("x", self.x_in, place.x, place.x_peer)
 
@@ -446,47 +424,36 @@
         self.y_in[place.y] = self.collect("x", self.x_in, place.x, place.x_peer)
         self.spread("y", self.y_in, place.y, place.y_peer)
 
-    def share(self, tile):
-        return self.total.at[pl.ds(self.place.core * self.half + tile * self.part, self.part)]
-
     def back(self):
         place = self.place
-        at = self.share(place.tile)
+        at = self.total.at[self.share(0, 0)]
         at[...] = self.collect("y", self.y_in, place.y, place.y_peer)
-        for k in range(1, self.tiles):
-            self.sender.send(("back", k), at, at, place.tile_peer(k, self.tiles))
-
-    def back_core(self):
-        place = self.place
-        for k in range(1, self.tiles):
-            source = (place.tile + self.tiles - k) % self.tiles
-            self.sender.arrive(("back", k), self.share(source), {"tile": source})
-        at = self.total.at[self.tiles_of(place.core)]
-        self.sender.send("other", at, at, place.other())
+        for other, k in self.others:
+            self.sender.send(("back", other, k), at, at, self.peer(other, k))
 
     def finish(self):
-        self.sender.arrive("other", self.total.at[self.tiles_of(1 - self.place.core)], self.place.other())
+        for other, k in self.others:
+            back = self.tiles - k
+            self.sender.arrive(("back", other, k), self.total.at[self.share(other, back)], self.peer(other, back))
         return self.total
 
 
 def gather_kernel(
-    object_hbm, amp_hbm, rows_hbm, cols_hbm, counts_hbm, out_hbm, amp_in, rows_in, cols_in, counts_in,
-    object_ref, mine, send_sem, recv_sem, copy_sem,
+    object_hbm, amp_hbm, rows_hbm, cols_hbm, counts_hbm, out_ref, amp_in, rows_in, cols_in, counts_in,
+    object_ref, send_sem, recv_sem, copy_sem,
 ):
     place = Place()
+    met = greet(place, 1)
     copy = pltpu.make_async_copy(object_hbm, object_ref, copy_sem)
     copy.start()
     copy.wait()
     for g in range(2):
         for p in range(2):
             for b in range(COLS):
-                mine[COLS * p + b, g] = object_ref[p, 8 * g : 8 * g + 8, WIN * b : WIN * b + WIN]
-    copy = pltpu.make_async_copy(mine, out_hbm.at[:, pl.ds(2 * place.at(0, 0), 2)], copy_sem)
-    copy.start()
-    greet(place, 1)
-    copy.wait()
+                out_ref[COLS * p + b, 2 * place.at(0, 0) + g] = object_ref[p, 8 * g : 8 * g + 8, WIN * b : WIN * b + WIN]
+    met()
     sender = Sender(send_sem, recv_sem)
-    strip = Gather(place, sender, out_hbm)
+    strip = Gather(place, sender, out_ref)
     strip.start(0)
     strip.start(1)
     other = place.other()
@@ -506,35 +473,27 @@
 
 
 def exchange_kernel(
-    tiles, last, sums_hbm, probe_src, strip_hbm, *refs,
+    tiles, last, sums_ref, probe_src, strip_ref, *refs,
 ):
     if last:
         probe_ref, object_out, probe_out = refs[:3]
         refs = refs[3:]
     else:
-        out_hbm, sums_out = refs[:2]
+        out_ref, sums_out = refs[:2]
         refs = refs[2:]
-    (old, own, core_in, far_in, near_in, relay_in, mine,
-     p_own, p_core, p_tile, p_x, p_y, p_total,
-     load_sem, copy_sem, send_sem, recv_sem, send_sem2, recv_sem2, send_sem3, recv_sem3) = refs
+    (own, core_in, far_in, near_in, relay_in,
+     p_tile, p_x, p_y, p_total,
+     send_sem, recv_sem, send_sem2, recv_sem2, send_sem3, recv_sem3) = refs
     place = Place()
-    here = pl.ds(2 * place.at(0, 0), 2)
-    load = pltpu.make_async_copy(strip_hbm.at[:, here], old, copy_sem.at[0])
-    load.start()
+    met = greet(place, tiles)
     first, second, third = Sender(send_sem, recv_sem), Sender(send_sem2, recv_sem2), Sender(send_sem3, recv_sem3)
-    sums = Reduce(place, first, sums_hbm, own, core_in, far_in, near_in, load_sem)
-    sums.relay_in = relay_in
-    probe = ProbeSum(
-        place, third, probe_src, tiles, p_own, p_core, p_tile, p_x, p_y, p_total, copy_sem.at[3]
-    )
-    probe.load()
-    sums.load()
-    greet(place, tiles)
-    probe.core()
+    sums = Reduce(place, first, sums_ref, own, core_in, far_in, near_in, relay_in)
+    probe = ProbeSum(place, third, probe_src, tiles, p_tile, p_x, p_y, p_total)
+    met()
+    probe.across()
     sums.core_send(0)
     sums.core_send(1)
     sums.far_first(0)
-    probe.across()
     sums.far_first(1)
     sums.far_second(0)
     probe.along_x()
@@ -542,30 +501,25 @@
     sums.near_send(0)
     probe.along_y()
     sums.near_send(1)
-    strip = None if last else Gather(place, second, out_hbm)
+    strip = None if last else Gather(place, second, out_ref)
 
     def step(h):
         total = sums.total(h)
-        if h == 0:
-            load.wait()
+        old = strip_ref[:, 2 * place.at(0, 0) + h]
         for b in range(COLS):
             scale = 1.0 / (total[2 * COLS + b] + 1.0)
             for p in range(2):
-                tile = (old[COLS * p + b, h] + total[COLS * p + b]) * scale
+                tile = (old[COLS * p + b] + total[COLS * p + b]) * scale
                 if last:
                     object_out[p, 8 * h : 8 * h + 8, WIN * b : WIN * b + WIN] = tile
                 else:
-                    mine[COLS * p + b, h] = tile
+                    out_ref[COLS * p + b, 2 * place.at(0, 0) + h] = tile
         if not last:
-            copy = pltpu.make_async_copy(mine.at[:, h], strip.at(h, 0, 0), copy_sem.at[1 + h])
-            copy.start()
-            copy.wait()
             strip.start(h)
 
     probe.back()
     step(0)
     step(1)
-    probe.back_core()
     if last:
         stepped = probe_step(probe_ref, probe.finish().reshape(3, WIN, WIN))
         for k in range(2):
@@ -597,9 +551,9 @@
         out_shape=[jax.ShapeDtypeStruct((OTILES, GROUPS, 8, WIN), f32), jax.ShapeDtypeStruct(halves, f32)]
         + [jax.ShapeDtypeStruct(array.shape, jnp.int32) for array in offsets],
         in_specs=[ANY] * 5,
-        out_specs=[ANY] * 5,
+        out_specs=[VMEM] + [ANY] * 4,
         scratch_shapes=[
-            pltpu.VMEM(object_field.shape, f32), pltpu.VMEM((OTILES, 2, 8, WIN), f32), dma(copies), dma(copies), pltpu.SemaphoreType.DMA,
+            pltpu.VMEM(object_field.shape, f32), dma(copies), dma(copies), pltpu.SemaphoreType.DMA,
         ],
         compiler_params=params(0),
         name="gather_object",
@@ -614,21 +568,20 @@
         out_specs = (VMEM, VMEM)
     else:
         out_shape = (jax.ShapeDtypeStruct(strip.shape, f32), jax.ShapeDtypeStruct((PTILES, 8, WIN), f32))
-        out_specs = (ANY, VMEM)
+        out_specs = (VMEM, VMEM)
     group, part = (STILES, 8, WIN), (PTILES // 2 // tiles, 8, WIN)
     buffers = [
-        (OTILES, 2, 8, WIN), (2, RING, RING) + group, (2, RING, RING) + group, (2, 3, RING) + group, (2, 3) + group,
-        (2, 2, RING, STILES // 2, 8, WIN), (OTILES, 2, 8, WIN),
-        (PTILES // 2, 8, WIN), (PTILES // 2, 8, WIN), (tiles - 1,) + part, (RING,) + part, (RING,) + part, (PTILES, 8, WIN),
+        (2, RING, RING) + group, (2, RING, RING) + group, (2, 3, RING) + group, (2, 3) + group,
+        (2, 2, RING, STILES // 2, 8, WIN),
+        (2 * tiles,) + part, (RING,) + part, (RING,) + part, (PTILES, 8, WIN),
     ]
     return pl.pallas_call(
         functools.partial(exchange_kernel, tiles, is_last),
         out_shape=out_shape,
-        in_specs=[ANY, ANY, ANY] + ([VMEM] if is_last else []),
+        in_specs=[VMEM] * (4 if is_last else 3),
         out_specs=out_specs,
         scratch_shapes=[pltpu.VMEM(shape, f32) for shape in buffers]
-        + [dma(2 * RING * RING), dma(4)]
-        + [dma(REDUCE_COPIES)] * 2 + [dma(GATHER_COPIES)] * 2 + [dma(8 + 2 * (tiles - 1))] * 2,
+        + [dma(REDUCE_COPIES)] * 2 + [dma(GATHER_COPIES)] * 2 + [dma(6 + 2 * (2 * tiles - 1))] * 2,
         compiler_params=params(2 if is_last else 1),
         name="exchange_last" if is_last else "exchange_middle",
     )(sums, probe_sums, strip, *([probe] if is_last else []))

time: 110 us -> 107 us (0.973)
  Pallas kernels: 108 us -> 104 us
    pallas_call x2, Pallas kernels: 77 us -> 70.1 us  [exchange(): pl.pallas_call(functools.partial(exchange_kernel, tiles, is_last), out_sh...]
    pallas_call x2, Pallas kernels: 11.2 us -> 15.1 us  [sweep(): pl.pallas_call(functools.partial(sweep_kernel, iteration, updates), out_s...]
where the time goes in v5:
time: 107 us; the launch traced here: 106 us
  Pallas kernels  104 us (97%)
  local copies, waits for them, and re-layouts  1.29 us (1%)
    pallas_call x2, Pallas kernels, exchange(): pl.pallas_call(functools.partial(exchange_kernel, tiles, is_last), out_sh...  70.1 us
    pallas_call x1, Pallas kernels, gather_object(): pl.pallas_call(gather_kernel, out_shape=[jax.ShapeDtypeStruct((OTILES, GR...  18.7 us
    pallas_call x2, Pallas kernels, sweep(): pl.pallas_call(functools.partial(sweep_kernel, iteration, updates), out_s...  15.1 us

profile of v5, /device:TPU:1, one launch (start us, length us, event | category | flops | bytes accessed | tf_op | source)
XLA Modules:
  0.0 105.9 jit_solution(8021210664280313111)
XLA Ops:
  0.6 18.7 %gather_object.1 = (f32[8,64,8,128]{3,2,1,0:T(8,128)S(1)}, f32[2,16,128,128]{3,2,1,0:T(8,128)S(1)}, s32[2,32]{1,0:T(2,128)S(1)}, s32[2,32]{1,0:T(2,128)S(1)}, s32[1,2]{1,0:T(1,128)S(1)}) custom-call(f32[2,16,512]{2,1,0:T(8,128)} %object_hbm.1, f32[2,16,2,128,128]{4,3,2,1,0:T(8,128)} %bitcast.2, s32[2,32]{1,0:T(2,128)} %rows_hbm.5, s32[2,32]{1,0:T(2,128)} %cols_hbm.5, ...), custom_call_target="tpu_custom_call" | custom-call | tf_op jit(solution)/shard_map/gather_object/pallas_call | solution.py:549
  19.3 6.0 %sweep.2 = (f32[12,64,8,128]{3,2,1,0:T(8,128)S(1)}, f32[48,8,128]{2,1,0:T(8,128)S(1)}, f32[2,128,128]{2,1,0:T(8,128)S(1)}) custom-call(s32[2,32]{1,0:T(2,128)} %rows_hbm.5, s32[2,32]{1,0:T(2,128)} %cols_hbm.5, s32[1,2]{1,0:T(1,128)} %bitcast.6, s32[2,32]{1,0:T(2,128)S(1)} %get-tuple-element.15.rows_in, s32[2,32]{1,0:T(2,128)S(1)} %get-tuple-element.16.cols_in, ...), custom_call_target="tpu_custom_call" | custom-call | tf_op jit(solution)/shard_map/sweep/pallas_call | solution.py:192
  25.4 40.4 %exchange_middle.1 = (f32[8,64,8,128]{3,2,1,0:T(8,128)S(1)}, f32[48,8,128]{2,1,0:T(8,128)S(1)}) custom-call(f32[12,64,8,128]{3,2,1,0:T(8,128)S(1)} %get-tuple-element.21.sums_ref, f32[48,8,128]{2,1,0:T(8,128)S(1)} %get-tuple-element.22.probe_src, f32[8,64,8,128]{3,2,1,0:T(8,128)S(1)} %get-tuple-element.18.strip.strip_ref), custom_call_target="tpu_custom_call" | custom-call | tf_op jit(solution)/shard_map/exchange_middle/pallas_call | solution.py:578
  65.8 9.0 %sweep.3 = (f32[12,64,8,128]{3,2,1,0:T(8,128)S(1)}, f32[48,8,128]{2,1,0:T(8,128)S(1)}, f32[2,128,128]{2,1,0:T(8,128)S(1)}) custom-call(s32[2,32]{1,0:T(2,128)} %rows_hbm.5, s32[2,32]{1,0:T(2,128)} %cols_hbm.5, s32[1,2]{1,0:T(1,128)} %bitcast.7, s32[2,32]{1,0:T(2,128)S(1)} %get-tuple-element.15.rows_in, s32[2,32]{1,0:T(2,128)S(1)} %get-tuple-element.16.cols_in, ...), custom_call_target="tpu_custom_call" | custom-call | tf_op jit(solution)/shard_map/sweep/pallas_call | solution.py:192
  74.8 29.7 %exchange_last.1 = (f32[2,16,512]{2,1,0:T(8,128)S(1)}, f32[2,128,128]{2,1,0:T(8,128)S(1)}) custom-call(f32[12,64,8,128]{3,2,1,0:T(8,128)S(1)} %get-tuple-element.25.sums_ref, f32[48,8,128]{2,1,0:T(8,128)S(1)} %get-tuple-element.26.probe_src, f32[8,64,8,128]{3,2,1,0:T(8,128)S(1)} %get-tuple-element.24.strip.strip_ref, ...), custom_call_target="tpu_custom_call" | custom-call | tf_op jit(solution)/shard_map/exchange_last/pallas_call | solution.py:578
  104.6 0.6 copy.11
  105.2 0.7 copy.12
